TPU v7x, 32 devices: a whole 2x2x4 slice. The times are simulated.
32 devices in a mesh: narrow: 2 (over core), wide: 16 (over z, y, x).
Axes of the slice: x: 2, y: 2, z: 4, core: 2. Of those that a mesh axis runs over, the one named last changes fastest.
Arguments:
- char_ids: int32 [32, 512, 50], P(('narrow', 'wide')), may hold values from 0 to 261
- word_lengths: int32 [32, 512], P(('narrow', 'wide')), may hold values from 1 to 50, as said below
- type_ids: int32 [32, 512], P(('narrow', 'wide')), may hold values from 0 to 1
- cotangent: bfloat16 [32, 512, 768], P(('narrow', 'wide')), may hold values from -6 to 6
- character_embedding_table: bfloat16 [262, 16], replicated, may hold values from -4 to 4
- conv_weight: bfloat16 [112, 2048], P(None, 'wide'), may hold values from -0.75 to 0.75
- conv_bias: bfloat16 [2048], P('wide'), may hold values from -1.75 to 1.75
- high_weight: bfloat16 [2, 2048, 4096], P(None, None, 'wide'), may hold values from -0.125 to 0.125
- high_bias: bfloat16 [2, 4096], P(None, 'wide'), may hold values from -1.75 to 1.75
- proj_weight: bfloat16 [2048, 768], P('wide'), may hold values from -0.25 to 0.25
- proj_bias: bfloat16 [768], P('wide'), may hold values from -1.75 to 1.75
- pos_table: bfloat16 [512, 768], P(None, 'wide'), may hold values from -3 to 3
- type_table: bfloat16 [2, 768], P(None, 'wide'), may hold values from -3 to 3
- embed_gain: bfloat16 [768], P('wide'), may hold values from 0.5 to 1.5
- embed_shift: bfloat16 [768], P('wide'), may hold values from -1.75 to 1.75
- qkv_weight: bfloat16 [768, 2304], P(None, 'wide'), may hold values from -0.21875 to 0.21875
- attn_bias: bfloat16 [1536], P('wide'), may hold values from -1.75 to 1.75
- out_weight: bfloat16 [768, 768], P('wide'), may hold values from -1.25 to 1.25
- out_bias: bfloat16 [768], P('wide'), may hold values from -1.75 to 1.75
- attn_gain: bfloat16 [768], P('wide'), may hold values from 0.5 to 1.5
- attn_shift: bfloat16 [768], P('wide'), may hold values from -1.75 to 1.75
- up_weight: bfloat16 [768, 3072], P(None, 'wide'), may hold values from -0.21875 to 0.21875
- up_bias: bfloat16 [3072], P('wide'), may hold values from -1.75 to 1.75
- down_weight: bfloat16 [3072, 768], P('wide'), may hold values from -0.109375 to 0.109375
- down_bias: bfloat16 [768], P('wide'), may hold values from -1.75 to 1.75
- ffn_gain: bfloat16 [768], P('wide'), may hold values from 0.5 to 1.5
- ffn_shift: bfloat16 [768], P('wide'), may hold values from -1.75 to 1.75
Outputs:
- hidden_out: bfloat16 [32, 512, 768], P(('narrow', 'wide'))
- grad_char_table: float32 [262, 16], replicated
- grad_conv_weight: float32 [112, 2048], P(None, ('narrow', 'wide'))
- grad_conv_bias: float32 [2048], P(('narrow', 'wide'))
- grad_high_weight: float32 [2, 2048, 4096], P(None, None, ('narrow', 'wide'))
- grad_high_bias: float32 [2, 4096], P(None, ('narrow', 'wide'))
- grad_proj_weight: float32 [2048, 768], P(('narrow', 'wide'))
- grad_proj_bias: float32 [768], P(('narrow', 'wide'))
- grad_pos_table: float32 [512, 768], P(None, ('narrow', 'wide'))
- grad_type_table: float32 [2, 768], P(None, ('narrow', 'wide'))
- grad_embed_gain: float32 [768], P(('narrow', 'wide'))
- grad_embed_shift: float32 [768], P(('narrow', 'wide'))
- grad_qkv_weight: float32 [768, 2304], P(None, ('narrow', 'wide'))
- grad_attn_bias: float32 [1536], P(('narrow', 'wide'))
- grad_out_weight: float32 [768, 768], P(('narrow', 'wide'))
- grad_out_bias: float32 [768], P(('narrow', 'wide'))
- grad_attn_gain: float32 [768], P(('narrow', 'wide'))
- grad_attn_shift: float32 [768], P(('narrow', 'wide'))
- grad_up_weight: float32 [768, 3072], P(None, ('narrow', 'wide'))
- grad_up_bias: float32 [3072], P(('narrow', 'wide'))
- grad_down_weight: float32 [3072, 768], P(('narrow', 'wide'))
- grad_down_bias: float32 [768], P(('narrow', 'wide'))
- grad_ffn_gain: float32 [768], P(('narrow', 'wide'))
- grad_ffn_shift: float32 [768], P(('narrow', 'wide'))
Inputs may be any that keep to these rules, and one draw needn't show every extreme that they name: `word_lengths`: every sequence holds at least one word of 50 characters.
All inputs are finite; a program needn't handle non-finite values.
Results may differ from a plain program's by a relative error of at most 0.017.
Values may be sent and summed in bfloat16 or wider, within the bound.
No kernel may reach another device: no remote copies, remote signals or barrier semaphores. Data moves between devices by JAX's collectives and lax.ppermute only.
A program may use at most 384 MiB of HBM per device.

v0:
```python
from functools import partial

import jax
import jax.numpy as jnp
from jax import lax
from jax.experimental import pallas as pl
from jax.experimental.pallas import tpu as pltpu
from jax.sharding import PartitionSpec as P

HEADS = 12
HEAD_DIM = 64
CHAR_DIM = 16
TAPS = 7
EPSILON = 1e-12

LANES = 128
GROUP = LANES // CHAR_DIM
BLOCK_WORDS = 32
CHUNK_BLOCKS = 16
CHUNK = BLOCK_WORDS * CHUNK_BLOCKS
TABLE_PAD = 384
ROW_TILE = 128
BIAS_LANE = TAPS * CHAR_DIM

F32 = jnp.float32
BF16 = jnp.bfloat16
VMEM = pl.BlockSpec(memory_space=pltpu.VMEM)
SMEM = pl.BlockSpec(memory_space=pltpu.SMEM)
MIB = 1024 * 1024


def cost(microseconds):
    return pl.CostEstimate(
        flops=int(microseconds * 1.1e9), bytes_accessed=int(microseconds * 3e6), transcendentals=0
    )


def dot(left, right):
    return lax.dot_general(left, right, (((1,), (0,)), ((), ())), preferred_element_type=F32)


def dot_nt(left, right):
    return lax.dot_general(left, right, (((1,), (1,)), ((), ())), preferred_element_type=F32)


def dot_tn(left, right):
    return lax.dot_general(left, right, (((0,), (0,)), ((), ())), preferred_element_type=F32)


def column_sum(values):
    return jnp.sum(values.astype(F32), axis=0)


def filter_widths(filter_count):
    column = jnp.arange(filter_count)
    widths = jnp.ones((filter_count,), jnp.int32)
    for exponent in range(6):
        widths = widths + (column >= filter_count * 2**exponent // 64).astype(jnp.int32)
    return widths


def sort_words(char_ids, lengths, groups):
    words, chars = char_ids.shape
    index = jnp.arange(words)
    longer = lengths[None, :] > lengths[:, None]
    tie = (lengths[None, :] == lengths[:, None]) & (index[None, :] < index[:, None])
    rank = jnp.sum((longer | tie).astype(jnp.int32), axis=1)
    perm = (rank[None, :] == index[:, None]).astype(BF16)
    live = jnp.arange(chars)[None, :] < lengths[:, None]
    shifted = jnp.where(live, char_ids + 1, 0)
    packed = jnp.concatenate(
        [shifted >> 4, shifted & 15, lengths[:, None]], axis=1
    ).astype(BF16)
    sorted_packed = dot(perm, packed).astype(jnp.int32)
    ids = (sorted_packed[:, :chars] << 4) + sorted_packed[:, chars : 2 * chars] - 1
    ids = jnp.pad(ids, ((0, 0), (0, GROUP * groups - chars)), constant_values=-1)
    sorted_lengths = sorted_packed[:, 2 * chars]
    tile_count = words // BLOCK_WORDS
    tile_max = jnp.max(sorted_lengths.reshape(tile_count, BLOCK_WORDS), axis=1)
    cum = jnp.cumsum(tile_max)
    total = cum[-1]
    block = jnp.arange(tile_count * chars + CHUNK_BLOCKS)
    tile = jnp.sum((block[:, None] >= cum[None, :]).astype(jnp.int32), axis=1)
    start = jnp.sum(
        jnp.where(tile[:, None] == jnp.arange(tile_count)[None, :], (cum - tile_max)[None, :], 0),
        axis=1,
    )
    valid = block < total
    position = jnp.where(valid, block - start, chars).astype(jnp.int32)
    tile = jnp.where(valid, tile, 0).astype(jnp.int32)
    chunks = (total + CHUNK_BLOCKS - 1) // CHUNK_BLOCKS
    reach = jnp.sum(
        (sorted_lengths[None, :] > GROUP * jnp.arange(groups - 1)[:, None]).astype(jnp.int32), axis=1
    )
    scalars = jnp.concatenate([chunks[None], (reach + ROW_TILE - 1) // ROW_TILE]).astype(jnp.int32)
    return perm, ids, sorted_lengths, scalars, tile, position


def build_windows(chunk, tile_ref, pos_ref, g_ref, len_ref, x_ref):
    lane = lax.broadcasted_iota(jnp.int32, (BLOCK_WORDS, LANES), 1)
    for b in range(CHUNK_BLOCKS):
        block = chunk * CHUNK_BLOCKS + b
        row = pl.multiple_of(tile_ref[block] * BLOCK_WORDS, BLOCK_WORDS)
        position = pos_ref[block]
        group = position >> 3
        offset = (position & 7) * CHAR_DIM
        shift = lax.rem(LANES - offset, LANES)
        here = pltpu.roll(g_ref[group, pl.ds(row, BLOCK_WORDS), :].astype(F32), shift, 1)
        after = pltpu.roll(g_ref[group + 1, pl.ds(row, BLOCK_WORDS), :].astype(F32), shift, 1)
        live = (len_ref[pl.ds(row, BLOCK_WORDS), :] > position).astype(F32)
        value = jnp.where(lane < LANES - offset, here, after)
        value = jnp.where(lane < BIAS_LANE, value, jnp.where(lane == BIAS_LANE, live, 0.0))
        x_ref[b * BLOCK_WORDS : (b + 1) * BLOCK_WORDS, :] = value.astype(BF16)


def embed_kernel(scalar_ref, ids_ref, table_ref, g_ref):
    groups = g_ref.shape[0]
    g_ref[...] = jnp.zeros_like(g_ref)
    identity = lax.broadcasted_iota(jnp.int32, (ROW_TILE, TABLE_PAD), 1)
    for group in range(groups - 1):

        def embed(step, carry, group=group):
            row = pl.multiple_of(step * ROW_TILE, ROW_TILE)
            total = jnp.zeros((ROW_TILE, LANES), F32)
            for k in range(GROUP):
                column = group * GROUP + k
                hot = (ids_ref[pl.ds(row, ROW_TILE), column : column + 1] == identity).astype(F32)
                total = total + dot(hot.astype(BF16), table_ref[k])
            g_ref[group, pl.ds(row, ROW_TILE), :] = total.astype(BF16)
            return carry

        lax.fori_loop(0, scalar_ref[1 + group], embed, 0)


def embed_characters(prep, table_blocks):
    _, ids, _, scalars, _, _ = prep
    return pl.pallas_call(
        embed_kernel,
        out_shape=jax.ShapeDtypeStruct((ids.shape[1] // GROUP, ids.shape[0], LANES), BF16),
        in_specs=[SMEM, VMEM, VMEM],
        out_specs=VMEM,
        compiler_params=pltpu.CompilerParams(vmem_limit_bytes=32 * MIB),
        cost_estimate=cost(5),
        name="embed",
    )(scalars, ids, table_blocks)


def conv_forward_kernel(
    scalar_ref, tile_ref, pos_ref, g_ref, w_ref, len_ref, pooled_ref, x_ref, pre_ref
):
    filters = w_ref.shape[1]
    part = pre_ref.shape[1]
    pooled_ref[...] = jnp.zeros_like(pooled_ref)

    def step(chunk, carry):
        build_windows(chunk, tile_ref, pos_ref, g_ref, len_ref, x_ref)
        for first in range(0, filters, part):
            half = dot(x_ref[...], w_ref[:, first : first + part])
            pre_ref[...] = half + half * jnp.tanh(half)
            for b in range(CHUNK_BLOCKS):
                row = pl.multiple_of(
                    tile_ref[chunk * CHUNK_BLOCKS + b] * BLOCK_WORDS, BLOCK_WORDS
                )
                pooled_ref[pl.ds(row, BLOCK_WORDS), first : first + part] += pre_ref[
                    b * BLOCK_WORDS : (b + 1) * BLOCK_WORDS, :
                ]
        return carry

    lax.fori_loop(0, scalar_ref[0], step, 0)
    pooled_ref[...] = pooled_ref[...] / len_ref[...].astype(F32)


def conv_forward(prep, char_groups, half_matrix):
    _, ids, lengths, scalars, tile, position = prep
    return pl.pallas_call(
        conv_forward_kernel,
        out_shape=jax.ShapeDtypeStruct((ids.shape[0], half_matrix.shape[1]), F32),
        in_specs=[SMEM, SMEM, SMEM, VMEM, VMEM, VMEM],
        out_specs=VMEM,
        scratch_shapes=[pltpu.VMEM((CHUNK, LANES), BF16), pltpu.VMEM((CHUNK, 512), F32)],
        compiler_params=pltpu.CompilerParams(vmem_limit_bytes=32 * MIB),
        cost_estimate=cost(16),
        name="conv_forward",
    )(scalars, tile, position, char_groups, half_matrix, lengths[:, None])


def conv_backward_kernel(
    scalar_ref, tile_ref, pos_ref, g_ref, w_ref, len_ref, gp_ref, out_ref, gg_ref, x_ref, d_ref, dw_ref
):
    filters = w_ref.shape[1]
    part = 512
    lane = lax.broadcasted_iota(jnp.int32, (BLOCK_WORDS, LANES), 1)
    dw_ref[...] = jnp.zeros_like(dw_ref)
    gg_ref[...] = jnp.zeros_like(gg_ref)

    def step(chunk, carry):
        build_windows(chunk, tile_ref, pos_ref, g_ref, len_ref, x_ref)
        for first in range(0, filters, part):
            columns = slice(first, first + part)
            half = dot(x_ref[...], w_ref[:, columns])
            tanh = jnp.tanh(half)
            slope = (1.0 + tanh) * (1.0 + (half - half * tanh))
            for b in range(CHUNK_BLOCKS):
                rows = slice(b * BLOCK_WORDS, (b + 1) * BLOCK_WORDS)
                row = pl.multiple_of(
                    tile_ref[chunk * CHUNK_BLOCKS + b] * BLOCK_WORDS, BLOCK_WORDS
                )
                d_ref[rows, columns] = (
                    gp_ref[pl.ds(row, BLOCK_WORDS), columns] * slope[rows]
                ).astype(BF16)
            dw_ref[:, columns] += dot_tn(x_ref[...], d_ref[:, columns])
        gx = dot_nt(d_ref[...], w_ref[...])
        for b in range(CHUNK_BLOCKS):
            block = chunk * CHUNK_BLOCKS + b
            row = pl.multiple_of(tile_ref[block] * BLOCK_WORDS, BLOCK_WORDS)
            position = pos_ref[block]
            group = position >> 3
            offset = (position & 7) * CHAR_DIM
            value = gx[b * BLOCK_WORDS : (b + 1) * BLOCK_WORDS, :]
            value = pltpu.roll(jnp.where(lane < BIAS_LANE, value, 0.0), offset, 1)
            gg_ref[group, pl.ds(row, BLOCK_WORDS), :] += jnp.where(lane >= offset, value, 0.0)
            gg_ref[group + 1, pl.ds(row, BLOCK_WORDS), :] += jnp.where(lane < offset, value, 0.0)
        return carry

    lax.fori_loop(0, scalar_ref[0], step, 0)
    out_ref[...] = dw_ref[...].T.astype(BF16)


def conv_backward(prep, char_groups, half_matrix, grad_scaled):
    _, ids, lengths, scalars, tile, position = prep
    filters = half_matrix.shape[1]
    return pl.pallas_call(
        conv_backward_kernel,
        out_shape=(
            jax.ShapeDtypeStruct((filters, LANES), BF16),
            jax.ShapeDtypeStruct(char_groups.shape, F32),
        ),
        in_specs=[SMEM, SMEM, SMEM, VMEM, VMEM, VMEM, VMEM],
        out_specs=(VMEM, VMEM),
        scratch_shapes=[
            pltpu.VMEM((CHUNK, LANES), BF16),
            pltpu.VMEM((CHUNK, filters), BF16),
            pltpu.VMEM((LANES, filters), F32),
        ],
        compiler_params=pltpu.CompilerParams(vmem_limit_bytes=48 * MIB),
        cost_estimate=cost(35),
        name="conv_backward",
    )(scalars, tile, position, char_groups, half_matrix, lengths[:, None], grad_scaled)


def table_kernel(scalar_ref, ids_ref, gg_ref, out_ref):
    groups = gg_ref.shape[0]
    out_ref[...] = jnp.zeros_like(out_ref)
    identity = lax.broadcasted_iota(jnp.int32, (TABLE_PAD, ROW_TILE), 0)
    for group in range(groups - 1):

        def step(index, carry, group=group):
            row = pl.multiple_of(index * ROW_TILE, ROW_TILE)
            grad = (2.0 * gg_ref[group, pl.ds(row, ROW_TILE), :]).astype(BF16)
            for k in range(GROUP):
                column = group * GROUP + k
                hot = (ids_ref[column : column + 1, pl.ds(row, ROW_TILE)] == identity).astype(F32)
                out_ref[k] += dot(hot.astype(BF16), grad)
            return carry

        lax.fori_loop(0, scalar_ref[1 + group], step, 0)


def table_gradient(prep, grad_groups, vocabulary):
    ids, scalars = prep[1], prep[3]
    total = pl.pallas_call(
        table_kernel,
        out_shape=jax.ShapeDtypeStruct((GROUP, TABLE_PAD, LANES), F32),
        in_specs=[SMEM, VMEM, VMEM],
        out_specs=VMEM,
        compiler_params=pltpu.CompilerParams(vmem_limit_bytes=32 * MIB),
        cost_estimate=cost(4),
        name="table",
    )(scalars, ids.T, grad_groups)
    parts = [total[k, :vocabulary, k * CHAR_DIM : (k + 1) * CHAR_DIM] for k in range(GROUP)]
    return sum(parts[1:], parts[0])


def table_lanes(table):
    padded = jnp.pad(table, ((0, TABLE_PAD - table.shape[0]), (0, 0)))
    return jnp.stack(
        [
            jnp.pad(padded, ((0, 0), (k * CHAR_DIM, LANES - (k + 1) * CHAR_DIM)))
            for k in range(GROUP)
        ]
    )


ANY = pl.BlockSpec(memory_space=pl.ANY)


def flat_pieces(pieces):
    return [array for half in pieces for chunk in half for array in chunk]


def piece_copies(layout, array, slot, first, own, pieces, whole_ref, sems, buffer):
    halves, chunks, arrays, rows = layout
    width = whole_ref.shape[2] // 2
    copies = []
    for half in range(halves):
        for chunk in range(chunks):
            ref = pieces[(half * chunks + chunk) * arrays + array]
            start = (own if half == 0 else 1 - own) * (chunks * rows) + chunk * rows
            start = pl.multiple_of(start, rows)
            for side in range(2):
                copies.append(
                    pltpu.make_async_copy(
                        ref.at[first if side == 0 else 1 - first, slot],
                        whole_ref.at[
                            buffer, pl.ds(start, rows), side * width : (side + 1) * width
                        ],
                        sems.at[buffer, len(copies)],
                    )
                )
    return copies


def fetch_pieces(layout, select_ref, own, pieces, whole_ref, sems):
    step = pl.program_id(0)

    def start(index):
        for array in range(layout[2]):

            @pl.when(index // 2 == array)
            def _(array=array):
                for copy in piece_copies(
                    layout, array, index % 2, select_ref[index], own, pieces, whole_ref, sems, index % 2
                ):
                    copy.start()

    @pl.when(step == 0)
    def _():
        start(0)

    @pl.when(step + 1 < pl.num_programs(0))
    def _():
        start(step + 1)

    buffer = step % 2
    for copy in piece_copies(layout, 0, 0, 0, own, pieces, whole_ref, sems, buffer):
        copy.wait()
    return buffer


def half_tanh(value):
    return 0.5 + 0.5 * jnp.tanh(0.5 * value)


def highway_forward_kernel(layout, place_ref, select_ref, core_ref, h_ref, bias_ref, *refs):
    count = layout[0] * layout[1] * layout[2]
    pieces = refs[:count]
    next_ref, transform_ref, gating_ref, low_ref, whole_ref, sems = refs[count:]
    step = pl.program_id(0)
    width = next_ref.shape[1]

    @pl.when(step == 0)
    def _():
        low_ref[...] = h_ref[...].astype(BF16)

    block = place_ref[step]
    blocks = bias_ref.shape[0] // 2
    buffer = fetch_pieces(layout, select_ref, core_ref[0], pieces, whole_ref, sems)
    mixed = dot(low_ref[...], whole_ref[buffer])
    transform = mixed[:, :width] + bias_ref[block]
    gating = half_tanh(mixed[:, width:] + bias_ref[block + blocks])
    h = h_ref[:, pl.ds(pl.multiple_of(block * width, width), width)]
    activated = transform * half_tanh(transform)
    transform_ref[...] = transform
    gating_ref[...] = gating
    next_ref[...] = activated + gating * (h - activated)


def highway_forward(h, pieces, bias_blocks, place, select, core):
    words, features = h.shape
    width = bias_blocks.shape[2]
    flat = flat_pieces(pieces)
    layout = (len(pieces), len(pieces[0]), len(pieces[0][0]), flat[0].shape[2])
    column = pl.BlockSpec((words, width), lambda j, place, *_: (0, place[j]))
    whole = lambda shape: pl.BlockSpec(shape, lambda j, *_: (0,) * len(shape))
    return pl.pallas_call(
        partial(highway_forward_kernel, layout),
        grid_spec=pltpu.PrefetchScalarGridSpec(
            num_scalar_prefetch=3,
            grid=(features // width,),
            in_specs=[whole(h.shape), whole(bias_blocks.shape)] + [ANY] * len(flat),
            out_specs=[column, column, column, whole(h.shape)],
            scratch_shapes=[
                pltpu.VMEM((2, features, 2 * width), BF16),
                pltpu.SemaphoreType.DMA((2, 2 * layout[0] * layout[1])),
            ],
        ),
        out_shape=(
            jax.ShapeDtypeStruct(h.shape, F32),
            jax.ShapeDtypeStruct(h.shape, F32),
            jax.ShapeDtypeStruct(h.shape, F32),
            jax.ShapeDtypeStruct(h.shape, BF16),
        ),
        compiler_params=pltpu.CompilerParams(vmem_limit_bytes=56 * MIB),
        cost_estimate=cost(19),
        name="highway_forward",
    )(place, select, core, h, bias_blocks, *flat)


def highway_backward_kernel(layout, place_ref, select_ref, core_ref, grad_ref, h_ref, t_ref, g_ref, *refs):
    count = layout[0] * layout[1] * layout[2]
    pieces = refs[:count]
    mixed_ref, sums_ref, out_ref, whole_ref, sems = refs[count:]
    step = pl.program_id(0)
    width = grad_ref.shape[1]
    features = out_ref.shape[1]

    @pl.when(step == 0)
    def _():
        out_ref[...] = jnp.zeros_like(out_ref)

    block = place_ref[step]
    buffer = fetch_pieces(layout, select_ref, core_ref[0], pieces, whole_ref, sems)
    grad = grad_ref[...]
    transform = t_ref[...]
    gating = g_ref[...]
    sigmoid = half_tanh(transform)
    activated = transform * sigmoid
    rest = grad * (1.0 - gating)
    low_t = (rest * (sigmoid + activated * (1.0 - sigmoid))).astype(BF16)
    low_g = (rest * gating * (h_ref[...] - activated)).astype(BF16)
    mixed_ref[0] = low_t
    mixed_ref[1] = low_g
    sums_ref[0] = jnp.sum(low_t.astype(F32), axis=0, keepdims=True)
    sums_ref[1] = jnp.sum(low_g.astype(F32), axis=0, keepdims=True)
    low = jnp.concatenate([low_t, low_g], axis=1)
    for start in range(0, features, 512):
        out_ref[:, start : start + 512] += dot_nt(
            low, whole_ref[buffer, start : start + 512, :]
        )
    out_ref[:, pl.ds(pl.multiple_of(block * width, width), width)] += grad * gating


def highway_backward(grad, h, transform, gating, pieces, place, select, core):
    words, features = h.shape
    flat = flat_pieces(pieces)
    width = flat[0].shape[3]
    layout = (len(pieces), len(pieces[0]), len(pieces[0][0]), flat[0].shape[2])
    column = pl.BlockSpec((words, width), lambda j, place, *_: (0, place[j]))
    return pl.pallas_call(
        partial(highway_backward_kernel, layout),
        grid_spec=pltpu.PrefetchScalarGridSpec(
            num_scalar_prefetch=3,
            grid=(features // width,),
            in_specs=[column] * 4 + [ANY] * len(flat),
            out_specs=[
                pl.BlockSpec((2, words, width), lambda j, place, *_: (0, 0, place[j])),
                pl.BlockSpec((2, 1, width), lambda j, place, *_: (0, 0, place[j])),
                pl.BlockSpec(h.shape, lambda j, *_: (0, 0)),
            ],
            scratch_shapes=[
                pltpu.VMEM((2, features, 2 * width), BF16),
                pltpu.SemaphoreType.DMA((2, 2 * layout[0] * layout[1])),
            ],
        ),
        out_shape=(
            jax.ShapeDtypeStruct((2, words, features), BF16),
            jax.ShapeDtypeStruct((2, 1, features), F32),
            jax.ShapeDtypeStruct(h.shape, F32),
        ),
        compiler_params=pltpu.CompilerParams(vmem_limit_bytes=56 * MIB),
        cost_estimate=cost(21),
        name="highway_backward",
    )(place, select, core, grad, h, transform, gating, *flat)


def weight_kernel(which_ref, left_ref, right_ref, *refs):
    out_ref = refs[-1]
    value = dot(left_ref[...], right_ref[0])
    width = out_ref.shape[2]
    for number in range(out_ref.shape[0]):
        block = value[:, number * width : (number + 1) * width]
        if len(refs) == 2:
            block = block + refs[0][number].astype(F32)
        out_ref[number] = block.astype(BF16)


def highway_weight_gradient(which, turned, mixed, first, rows, width, added=None, part=0):
    words, features = mixed.shape[1:]
    blocks = 8
    out = pl.BlockSpec((blocks, rows, width), lambda j, which: (j, 0, 0))
    return pl.pallas_call(
        weight_kernel,
        grid_spec=pltpu.PrefetchScalarGridSpec(
            num_scalar_prefetch=1,
            grid=(features // (blocks * width),),
            in_specs=[
                pl.BlockSpec((rows, words), lambda j, which: (first // rows, 0)),
                pl.BlockSpec((1, words, blocks * width), lambda j, which: (which[0], 0, j)),
            ]
            + (
                []
                if added is None
                else [pl.BlockSpec((blocks, rows, width), lambda j, which: (j, part, 0))]
            ),
            out_specs=out,
        ),
        out_shape=jax.ShapeDtypeStruct((features // width, rows, width), BF16),
        compiler_params=pltpu.CompilerParams(vmem_limit_bytes=32 * MIB),
        cost_estimate=cost(3),
        name="highway_weight",
    )(which, turned, mixed, *([] if added is None else [added]))


def turn_kernel(value_ref, out_ref):
    out_ref[...] = value_ref[...].T.astype(BF16)


def turn(value):
    rows, columns = value.shape
    return pl.pallas_call(
        turn_kernel,
        grid=(columns // 256,),
        in_specs=[pl.BlockSpec((rows, 256), lambda j: (0, j))],
        out_specs=pl.BlockSpec((256, rows), lambda j: (j, 0)),
        out_shape=jax.ShapeDtypeStruct((columns, rows), BF16),
        compiler_params=pltpu.CompilerParams(vmem_limit_bytes=32 * MIB),
        cost_estimate=cost(1),
        name="turn",
    )(value)


def place_rows_kernel(splits, place_ref, core_ref, *refs):
    arrays = (len(refs) - len(splits) - 1) // 2
    own_refs, other_refs = refs[:arrays], refs[arrays : 2 * arrays]
    out_refs, whole_ref = refs[2 * arrays : -1], refs[-1]
    step = pl.program_id(0)
    half_rows = own_refs[0].shape[1]
    core = core_ref[0]
    for array in range(arrays):

        @pl.when(step // 4 == array)
        def _(array=array):
            align = lambda start: pl.ds(pl.multiple_of(start, 16), half_rows)
            whole_ref[align(core * half_rows), :] = own_refs[array][0]
            whole_ref[align((1 - core) * half_rows), :] = other_refs[array][0]

    start = 0
    for rows, out_ref in zip(splits, out_refs):
        out_ref[...] = whole_ref[start : start + rows, :]
        start += rows


def place_rows(own, other, place, core, splits):
    half_rows, columns = own[0].shape[1:]

    def index(number):
        return lambda j, *_: (jnp.clip(j - 4 * number, 0, 3), 0, 0)

    specs = [pl.BlockSpec((1, half_rows, columns), index(number)) for number in range(len(own))]
    return pl.pallas_call(
        partial(place_rows_kernel, splits),
        grid_spec=pltpu.PrefetchScalarGridSpec(
            num_scalar_prefetch=2,
            grid=(4 * len(own),),
            in_specs=specs + specs,
            out_specs=[
                pl.BlockSpec((rows, columns), lambda j, place, *_: (place[j], 0)) for rows in splits
            ],
            scratch_shapes=[pltpu.VMEM((2 * half_rows, columns), BF16)],
        ),
        out_shape=[
            jax.ShapeDtypeStruct((4 * len(own) * rows, columns), BF16) for rows in splits
        ],
        compiler_params=pltpu.CompilerParams(vmem_limit_bytes=32 * MIB),
        cost_estimate=cost(7),
        name="place_rows",
    )(place, core, *own, *other)


def place_small_kernel(place_ref, *refs):
    inputs, (conv_ref, *row_refs) = refs[:4], refs[4:]
    step = pl.program_id(0)
    for number, ref in enumerate(inputs):

        @pl.when(step // 4 == number)
        def _(ref=ref):
            start = conv_ref.shape[0]
            conv_ref[...] = ref[0, :start, :]
            for row_ref in row_refs:
                row_ref[0] = ref[0, start : start + row_ref.shape[1], :]
                start += row_ref.shape[1]


def place_small(arrays, place, conv_rows, splits):
    rows, columns = arrays[0].shape[1:]

    def index(number):
        return lambda j, *_: (jnp.clip(j - 4 * number, 0, 3), 0, 0)

    return pl.pallas_call(
        place_small_kernel,
        grid_spec=pltpu.PrefetchScalarGridSpec(
            num_scalar_prefetch=1,
            grid=(16,),
            in_specs=[pl.BlockSpec((1, rows, columns), index(number)) for number in range(4)],
            out_specs=[pl.BlockSpec((conv_rows, columns), lambda j, place: (0, place[j]))]
            + [
                pl.BlockSpec((1, count, columns), lambda j, place: (place[j], 0, 0))
                for count in splits
            ],
        ),
        out_shape=[jax.ShapeDtypeStruct((conv_rows, 16 * columns), BF16)]
        + [jax.ShapeDtypeStruct((16, count, columns), BF16) for count in splits],
        compiler_params=pltpu.CompilerParams(vmem_limit_bytes=32 * MIB),
        cost_estimate=cost(2),
        name="place_small",
    )(place, *arrays)


LINKS = {
    "x": [(w, w ^ 1) for w in range(16)],
    "y": [(w, w ^ 2) for w in range(16)],
    "z": [(w, (w + 4) % 16) for w in range(16)],
    "back": [(w, (w - 4) % 16) for w in range(16)],
    "z1": [(w, w ^ 4) for w in range(16)],
    "z2": [(w, w ^ 8) for w in range(16)],
}
CORES = [(0, 1), (1, 0)]


def send(value, link):
    if link == "c":
        return lax.ppermute(value, "narrow", CORES)
    return lax.ppermute(value, "wide", LINKS[link])


def total_of(terms):
    return sum((term.astype(F32) for term in terms[1:]), terms[0].astype(F32))


class Exchange:
    windows = True

    def __init__(self):
        self.core = lax.axis_index("narrow")
        index = lax.axis_index("wide")
        self.z, self.y, self.x = index // 4, (index // 2) % 2, index % 2
        self.state, self.fresh, self.count, self.planned = {}, [], 0, []

    def put(self, key, value):
        self.state[key] = value
        self.fresh.append(key)

    def move(self, key, source, link):
        self.put(key, send(self.state[source], link))

    def plan(self, key, value, link, shape=None):
        self.planned.append((key, value, link, shape))

    def plan_move(self, source, *links):
        for link in links:
            self.plan(source + link, self.state[source], link)

    def plan_ring(self, name, step):
        self.plan(f"{name}r{step}", self.state[f"{name}r{step - 1}" if step > 1 else name], "z")

    def plan_swap(self, *names):
        for name in names:
            self.plan(name + "c", self.state[name], "c")

    def launch(self, values):
        leaves, tree = jax.tree.flatten(values)
        held = lax.optimization_barrier(
            tuple(value for _, value, _, _ in self.planned) + tuple(leaves)
        )
        for (key, _, link, shape), value in zip(self.planned, held):
            value = send(value, link)
            self.put(key, value if shape is None else value.reshape(shape))
        leaves = held[len(self.planned) :]
        self.planned = []
        return jax.tree.unflatten(tree, leaves)

    def window(self, values, hold=()):
        held_keys = [key for key in self.fresh if key in hold]
        self.fresh = [key for key in self.fresh if key not in hold]
        leaves, tree = jax.tree.flatten(values)
        held = lax.optimization_barrier(
            tuple(self.state[key] for key in self.fresh) + tuple(leaves)
        )
        for key, value in zip(self.fresh, held):
            self.state[key] = value
        leaves = held[len(self.fresh) :]
        self.fresh = held_keys
        return jax.tree.unflatten(tree, leaves)

    def swap_chain(self, *names):
        before = None
        for name in names:
            value = self.state[name]
            if before is not None:
                value, self.state[before] = lax.optimization_barrier((value, self.state[before]))
            before = name + "c"
            self.put(before, send(value, "c"))

    def stage(self, values=(), hold=()):
        return self.window(self.launch(values), hold)


    def load(self, name, value, rows=None, offset=0, whole=False):
        if not whole:
            rows = rows or value.shape[0] // 2
            value = lax.dynamic_slice_in_dim(
                value, self.core * (value.shape[0] // 2) + offset, rows, 0
            )
        self.state[name] = value

    def ring(self, name):
        received = [self.state[name]]
        for _ in range(3):
            received.append(send(received[-1], "z"))
        self.put(name + "o", jnp.stack(received))

    def ring_step(self, name, step):
        self.move(f"{name}r{step}", f"{name}r{step - 1}" if step > 1 else name, "z")

    def ring_both(self, name):
        self.put(name + "r1", send(self.state[name], "z"))
        self.put(name + "r3", send(self.state[name], "back"))
        self.put(name + "r2", send(self.state[name + "r1"], "z"))

    def ring_done(self, name):
        self.state[name + "o"] = jnp.stack(
            [self.state[name]] + [self.state[f"{name}r{step}"] for step in (1, 2, 3)]
        )

    def square(self, name):
        value = self.state[name]
        over_x = send(value, "x")
        self.put(name + "o0", jnp.stack([value, over_x, send(value, "y"), send(over_x, "y")]))

    def turn_ring(self, name, step):
        self.move(f"{name}o{step}", f"{name}o{step - 1}", "z")

    def swap(self, *names):
        for name in names:
            self.move(name + "c", name, "c")

    def near(self, name, suffix=""):
        return [self.state[name + part + suffix] for part in ("o", "ox", "oy", "oxy")]

    def layer(self, name, chunks):
        halves = []
        for suffix in ("", "c"):
            halves.append(
                [
                    [
                        array.reshape((2, 2) + array.shape[1:])
                        for array in self.near(f"{name}{chunk}", suffix)
                    ]
                    for chunk in range(chunks)
                ]
            )
        return halves

    def place(self, ring_last):
        step = jnp.arange(16)
        near, slot = (step % 4, step // 4) if ring_last else (step // 4, step % 4)
        return (
            (self.z - slot) % 4 * 4 + (self.y ^ (near >> 1)) * 2 + (self.x ^ (near & 1))
        ).astype(jnp.int32)

    def rows(self, own, other, splits, ring_last):
        core = self.core[None].astype(jnp.int32)
        return place_rows(own, other, self.place(ring_last), core, splits)


    def split(self, grads):
        blocks = [grad.astype(BF16).reshape(2, 16, -1, grad.shape[1]) for grad in grads]
        return tuple(
            jnp.concatenate(
                [lax.dynamic_index_in_dim(block, which, 0, keepdims=False) for block in blocks],
                axis=1,
            )
            for which in (self.core, 1 - self.core)
        )


class Reduction:
    def __init__(self, net, keep, sent, order):
        shape = (4, 2, 2) + keep.shape[1:]
        self.net, self.order, self.done = net, list(order), 0
        net.count += 1
        self.name = f"sum{net.count}"
        self.terms = [keep.reshape(shape)]
        self.keys, self.running, self.axes = [], None, ["z", "y", "x"]
        self.sent, self.shape = sent, shape

    def all_terms(self):
        return self.terms + [self.net.state[key] for key in self.keys]

    def pick(self, terms, index, axis):
        return [lax.dynamic_index_in_dim(term, index, axis, keepdims=False) for term in terms]

    def keep_only(self, index, axis):
        self.terms = self.pick(self.all_terms(), index, axis)
        self.keys = []

    def step(self, put=None):
        net, link = self.net, self.order[self.done]
        put = put or (lambda key, value, link, shape=None: net.put(
            key, send(value, link) if shape is None else send(value, link).reshape(shape)
        ))
        self.key = key = f"{self.name}_{self.done}"
        self.done += 1
        if link == "c":
            put(key, self.sent, "c", self.shape)
            self.keys.append(key)
        elif link in ("x", "y"):
            axis = self.axes.index(link)
            index = net.x if link == "x" else net.y
            sent = total_of(self.pick(self.all_terms(), 1 - index, axis)).astype(BF16)
            self.keep_only(index, axis)
            self.axes.remove(link)
            put(key, sent, link)
            self.keys.append(key)
        else:
            axis = self.axes.index("z")
            index = (net.z + int(link)) % 4
            terms = self.pick(self.all_terms(), index, axis)
            if self.running is not None:
                terms.append(net.state[self.running])
            put(key, total_of(terms).astype(BF16), "z")
            self.running = key
            if link == "1":
                self.keep_only(net.z, axis)
                self.axes.remove("z")
                self.keys = [key]
        return self

    def result(self):
        assert self.done == len(self.order)
        return total_of(self.all_terms())


class Ring:
    def __init__(self, net, sums, both):
        self.net, self.sums, self.both, self.done = net, sums, both, 0
        self.arrived = []
        net.count += 1
        self.name = f"ring{net.count}"

    def part(self, distance):
        index = (self.net.z + distance) % 4
        parts = [total_of(item.pick(item.all_terms(), index, 0)) for item in self.sums]
        value = parts[0] if len(parts) == 1 else jnp.concatenate(parts, axis=0)
        for key in self.arrived:
            value = value + self.net.state[key].astype(F32)
        return value

    def step(self, put):
        self.done += 1
        self.key = key = f"{self.name}_{self.done}"
        if self.both and self.done == 1:
            self.last_key = f"{self.name}_back"
            put(self.last_key, self.part(3).astype(BF16), "back")
            put(key, self.part(2).astype(BF16), "z")
        else:
            put(key, self.part((3 if self.both else 4) - self.done).astype(BF16), "z")
        self.arrived = [key]
        return self

    def result(self):
        assert self.done == (2 if self.both else 3)
        if self.both:
            self.arrived = self.arrived + [self.last_key]
        return self.part(0)


class Small:
    def __init__(self, net, value):
        self.net, self.value, self.done, self.key = net, value, 0, None
        net.count += 1
        self.name = f"t{net.count}"

    def result(self):
        return self.value if self.key is None else self.value + self.net.state[self.key]

    def step(self, put):
        self.value = self.result()
        self.key = f"{self.name}_{self.done}"
        put(self.key, self.value, ("c", "z1", "x", "y", "z2")[self.done])
        self.done += 1
        return self


class PlainReduction:
    def __init__(self, grads, axis):
        self.grads, self.axis = grads, axis

    def step(self):
        return self

    def result(self):
        return [
            lax.psum_scatter(
                grad.astype(BF16), ("narrow", "wide"), scatter_dimension=self.axis, tiled=True
            ).astype(F32)
            for grad in self.grads
        ]


def norm_rows(value, norm_gain, norm_shift):
    center = jnp.mean(value, axis=-1, keepdims=True)
    offsets = value - center
    spread = jnp.mean(offsets * offsets, axis=-1, keepdims=True)
    return offsets * lax.rsqrt(spread + EPSILON) * norm_gain + norm_shift


def norm_back(value, norm_gain, grad_rows):
    center = jnp.mean(value, axis=-1, keepdims=True)
    offsets = value - center
    spread = jnp.mean(offsets * offsets, axis=-1, keepdims=True)
    scale = lax.rsqrt(spread + EPSILON)
    normal = offsets * scale
    inner = grad_rows * norm_gain
    grad = scale * (
        inner
        - jnp.mean(inner, axis=-1, keepdims=True)
        - normal * jnp.mean(inner * normal, axis=-1, keepdims=True)
    )
    return grad, jnp.sum(grad_rows * normal, axis=0), jnp.sum(grad_rows, axis=0)


def array_copies(array, refs, held_ref, sems):
    count = len(refs)
    return [
        pltpu.make_async_copy(
            refs[index], held_ref.at[index], sems.at[index]
        )
        for index in range(array, count, count // 4)
    ]


def join_rows(slot_ref, own, refs, held_ref, up_ref, down_ref, sems):
    count = len(refs)
    arrays = count // 4
    step = pl.program_id(0)

    @pl.when(step == 0)
    def _():
        for array in range(arrays):
            for copy in array_copies(array, refs, held_ref, sems):
                copy.start()

    for array in range(arrays):

        @pl.when(step == 2 * array)
        def _(array=array):
            for copy in array_copies(array, refs, held_ref, sems):
                copy.wait()

    rows = held_ref.shape[2]
    near = step // 2
    for number in range(2):
        slot = slot_ref[step, number]
        for half in range(2):
            start = (own if half == 0 else 1 - own) * rows + number * 2 * rows
            where = pl.ds(pl.multiple_of(start, rows), rows)
            up_ref[where, :] = held_ref[half * arrays + near, slot]
            down_ref[where, :] = held_ref[(2 + half) * arrays + near, slot]


def normal_share(value, bell):
    t = 1.0 / (1.0 + (0.3275911 * 2**-0.5) * jnp.abs(value))
    series = 1.061405429
    for term in (-1.453152027, 1.421413741, -0.284496736, 0.254829592):
        series = series * t + term
    tail = (0.5 * series) * (t * bell)
    return jnp.where(value < 0.0, tail, 1.0 - tail)


def feed_forward_kernel(
    count, slot_ref, block_ref, core_ref, first_ref, bias_ref, vectors_ref, cotangent_ref, *refs
):
    (
        act_ref,
        slope_ref,
        hidden_ref,
        grad_ref,
        sums_ref,
        held_ref,
        up_ref,
        down_ref,
        low_ref,
        total_ref,
        sems,
    ) = refs[2 * count :]
    step = pl.program_id(0)

    @pl.when(step == 0)
    def _():
        low_ref[...] = first_ref[...].astype(BF16)
        total_ref[...] = first_ref[...] + vectors_ref[0:1, :]

    join_rows(slot_ref, core_ref[0], refs[: 2 * count], held_ref, up_ref, down_ref, sems)
    inner = dot_nt(low_ref[...], up_ref[...]) + bias_ref[block_ref[step]]
    bell = jnp.exp(-0.5 * inner * inner)
    share = normal_share(inner, bell)
    act = (inner * share).astype(BF16)
    act_ref[0] = act
    slope_ref[0] = (
        share + inner * (bell * (2.0 * jnp.pi) ** -0.5)
    ).astype(BF16)
    total_ref[...] += dot(act, down_ref[...])

    @pl.when(step == pl.num_programs(0) - 1)
    def _():
        value = total_ref[...]
        gain, shift = vectors_ref[1:2, :], vectors_ref[2:3, :]
        offsets = value - jnp.mean(value, axis=-1, keepdims=True)
        scale = lax.rsqrt(jnp.mean(offsets * offsets, axis=-1, keepdims=True) + EPSILON)
        normal = offsets * scale
        hidden_ref[...] = (normal * gain + shift).astype(BF16)
        cotangent = cotangent_ref[...].astype(F32)
        pulled = cotangent * gain
        grad = scale * (
            pulled
            - jnp.mean(pulled, axis=-1, keepdims=True)
            - normal * jnp.mean(pulled * normal, axis=-1, keepdims=True)
        )
        grad_ref[...] = grad
        sums_ref[0:1, :] = jnp.sum(cotangent * normal, axis=0, keepdims=True)
        sums_ref[1:2, :] = jnp.sum(cotangent, axis=0, keepdims=True)
        sums_ref[2:3, :] = jnp.sum(grad.astype(BF16).astype(F32), axis=0, keepdims=True)
        sums_ref[3:8, :] = jnp.zeros((5, sums_ref.shape[1]), F32)


def feed_forward(first, pieces, bias_blocks, vectors, cotangent, slots, block, core):
    words, columns = first.shape
    steps, width = bias_blocks.shape[0], bias_blocks.shape[2]
    up, down = pieces
    whole = lambda shape: pl.BlockSpec(shape, lambda j, *_: (0,) * len(shape))
    tile = pl.BlockSpec((1, words, width), lambda j, *_: (j, 0, 0))
    return pl.pallas_call(
        partial(feed_forward_kernel, len(up)),
        grid_spec=pltpu.PrefetchScalarGridSpec(
            num_scalar_prefetch=3,
            grid=(steps,),
            in_specs=[
                whole(first.shape),
                whole(bias_blocks.shape),
                whole(vectors.shape),
                whole(cotangent.shape),
            ]
            + [ANY] * (len(up) + len(down)),
            out_specs=[tile, tile, whole(first.shape), whole(first.shape), whole((8, columns))],
            scratch_shapes=[
                pltpu.VMEM((len(up) + len(down),) + up[0].shape, BF16),
                pltpu.VMEM((width, columns), BF16),
                pltpu.VMEM((width, columns), BF16),
                pltpu.VMEM((words, columns), BF16),
                pltpu.VMEM((words, columns), F32),
                pltpu.SemaphoreType.DMA((len(up) + len(down),)),
            ],
        ),
        out_shape=(
            jax.ShapeDtypeStruct((steps, words, width), BF16),
            jax.ShapeDtypeStruct((steps, words, width), BF16),
            jax.ShapeDtypeStruct((words, columns), BF16),
            jax.ShapeDtypeStruct((words, columns), F32),
            jax.ShapeDtypeStruct((8, columns), F32),
        ),
        compiler_params=pltpu.CompilerParams(vmem_limit_bytes=56 * MIB),
        cost_estimate=cost(20),
        name="feed_forward",
    )(slots, block, core, first, bias_blocks, vectors, cotangent, *up, *down)


def feed_forward_back_kernel(
    count,
    slot_ref,
    block_ref,
    core_ref,
    grad_ref,
    first_ref,
    act_ref,
    slope_ref,
    value_ref,
    gain_ref,
    *refs,
):
    (
        up_keep_ref,
        up_sent_ref,
        down_keep_ref,
        down_sent_ref,
        bias_ref,
        out_ref,
        sums_ref,
        held_ref,
        up_ref,
        down_ref,
        low_ref,
        low_first_ref,
        total_ref,
        sems,
    ) = refs[2 * count :]
    step = pl.program_id(0)

    @pl.when(step == 0)
    def _():
        total_ref[...] = grad_ref[...]
        low_ref[...] = grad_ref[...].astype(BF16)
        low_first_ref[...] = first_ref[...].astype(BF16)

    join_rows(slot_ref, core_ref[0], refs[: 2 * count], held_ref, up_ref, down_ref, sems)
    low = low_ref[...]
    inner = (dot_nt(low, down_ref[...]) * slope_ref[0].astype(F32)).astype(BF16)
    bias_ref[0] = jnp.sum(inner.astype(F32), axis=0, keepdims=True)
    grad_down = dot_tn(act_ref[0], low).astype(BF16)
    grad_up = dot_tn(inner, low_first_ref[...]).astype(BF16)
    total_ref[...] += dot(inner, up_ref[...])
    rows = up_keep_ref.shape[3]

    def store(value, ref):
        for number in range(4):
            ref[number // 2, 0, number % 2] = value[number * rows : (number + 1) * rows, :]

    @pl.when(step % 2 == 0)
    def _():
        store(grad_up, up_sent_ref)
        store(grad_down, down_sent_ref)

    @pl.when(step % 2 == 1)
    def _():
        store(grad_up, up_keep_ref)
        store(grad_down, down_keep_ref)

    @pl.when(step == pl.num_programs(0) - 1)
    def _():
        value = value_ref[...]
        pulling = total_ref[...]
        offsets = value - jnp.mean(value, axis=-1, keepdims=True)
        scale = lax.rsqrt(jnp.mean(offsets * offsets, axis=-1, keepdims=True) + EPSILON)
        normal = offsets * scale
        pulled = pulling * gain_ref[...]
        grad = scale * (
            pulled
            - jnp.mean(pulled, axis=-1, keepdims=True)
            - normal * jnp.mean(pulled * normal, axis=-1, keepdims=True)
        )
        out_ref[...] = grad
        sums_ref[0:1, :] = jnp.sum(pulling * normal, axis=0, keepdims=True)
        sums_ref[1:2, :] = jnp.sum(pulling, axis=0, keepdims=True)
        sums_ref[2:3, :] = jnp.sum(grad.astype(BF16).astype(F32), axis=0, keepdims=True)
        sums_ref[3:8, :] = jnp.zeros((5, sums_ref.shape[1]), F32)


def feed_forward_back(grad, first, act, slope, value, gain, pieces, slots, block, core):
    words, columns = first.shape
    steps, _, width = act.shape
    up, down = pieces
    rows = width // 4
    whole = lambda shape: pl.BlockSpec(shape, lambda j, *_: (0,) * len(shape))
    tile = pl.BlockSpec((1, words, width), lambda j, *_: (j, 0, 0))
    out = pl.BlockSpec(
        (2, 1, 2, rows, columns), lambda j, slots, block, core: (0, block[j] % (steps // 2), 0, 0, 0)
    )
    part = jax.ShapeDtypeStruct((2, steps // 2, 2, rows, columns), BF16)
    return pl.pallas_call(
        partial(feed_forward_back_kernel, len(up)),
        grid_spec=pltpu.PrefetchScalarGridSpec(
            num_scalar_prefetch=3,
            grid=(steps,),
            in_specs=[
                whole(grad.shape),
                whole(first.shape),
                tile,
                tile,
                whole(value.shape),
                whole(gain.shape),
            ]
            + [ANY] * (len(up) + len(down)),
            out_specs=[
                out,
                out,
                out,
                out,
                pl.BlockSpec((1, 1, width), lambda j, slots, block, core: (block[j], 0, 0)),
                whole(first.shape),
                whole((8, columns)),
            ],
            scratch_shapes=[
                pltpu.VMEM((len(up) + len(down),) + up[0].shape, BF16),
                pltpu.VMEM((width, columns), BF16),
                pltpu.VMEM((width, columns), BF16),
                pltpu.VMEM((words, columns), BF16),
                pltpu.VMEM((words, columns), BF16),
                pltpu.VMEM((words, columns), F32),
                pltpu.SemaphoreType.DMA((len(up) + len(down),)),
            ],
        ),
        out_shape=(
            part,
            part,
            part,
            part,
            jax.ShapeDtypeStruct((steps, 1, width), F32),
            jax.ShapeDtypeStruct((words, columns), F32),
            jax.ShapeDtypeStruct((8, columns), F32),
        ),
        compiler_params=pltpu.CompilerParams(vmem_limit_bytes=56 * MIB),
        cost_estimate=cost(25),
        name="feed_back",
    )(slots, block, core, grad, first, act, slope, value, gain, *up, *down)


def softmax_parts(query, key):
    scores = dot_nt(query, key)
    scaling = HEAD_DIM ** (-0.5) * 1.4426950408889634
    exponent = jnp.exp2((scores - jnp.max(scores, axis=-1, keepdims=True)) * scaling)
    return exponent, 1.0 / jnp.sum(exponent, axis=-1, keepdims=True)


def attend_kernel(query_ref, key_ref, value_ref, out_ref):
    for start in range(0, LANES, HEAD_DIM):
        head = slice(start, start + HEAD_DIM)
        exponent, scale = softmax_parts(query_ref[:, head], key_ref[:, head])
        attention = (exponent * scale).astype(BF16)
        out_ref[:, head] = dot(attention, value_ref[:, head]).astype(BF16)


def third(number, words, thirds):
    return pl.BlockSpec((words, LANES), lambda j: (0, number * thirds + j))


def attend(qkv):
    words = qkv.shape[0]
    pairs = qkv.shape[1] // (3 * LANES)
    return pl.pallas_call(
        attend_kernel,
        grid=(pairs,),
        in_specs=[third(number, words, pairs) for number in range(3)],
        out_specs=third(0, words, pairs),
        out_shape=jax.ShapeDtypeStruct((words, pairs * LANES), BF16),
        compiler_params=pltpu.CompilerParams(vmem_limit_bytes=32 * MIB),
        cost_estimate=cost(12),
        name="attend",
    )(qkv, qkv, qkv)


def attend_back_kernel(
    query_ref, key_ref, value_ref, grad_ref, grad_query_ref, grad_key_ref, grad_value_ref
):
    scaling = HEAD_DIM ** (-0.5)
    for start in range(0, LANES, HEAD_DIM):
        head = slice(start, start + HEAD_DIM)
        query, key = query_ref[:, head], key_ref[:, head]
        grad = grad_ref[:, head]
        exponent, scale = softmax_parts(query, key)
        attention = exponent * scale
        grad_attention = dot_nt(grad, value_ref[:, head])
        inner = jnp.sum(grad_attention * attention, axis=-1, keepdims=True)
        grad_scores = (attention * (grad_attention - inner)).astype(BF16)
        grad_value_ref[:, head] = dot_tn(attention.astype(BF16), grad).astype(BF16)
        grad_query_ref[:, head] = (dot(grad_scores, key) * scaling).astype(BF16)
        grad_key_ref[:, head] = (dot_tn(grad_scores, query) * scaling).astype(BF16)


def attend_back(qkv, grad_context):
    words = qkv.shape[0]
    pairs = qkv.shape[1] // (3 * LANES)
    out = third(0, words, pairs)
    return jnp.concatenate(
        pl.pallas_call(
            attend_back_kernel,
            grid=(pairs,),
            in_specs=[third(number, words, pairs) for number in range(3)] + [out],
            out_specs=(out, out, out),
            out_shape=(jax.ShapeDtypeStruct(grad_context.shape, BF16),) * 3,
            compiler_params=pltpu.CompilerParams(vmem_limit_bytes=32 * MIB),
            cost_estimate=cost(17),
        name="attend_back",
        )(qkv, qkv, qkv, grad_context),
        axis=1,
    )


def gather_plain(value, axis):
    return lax.all_gather(value, "wide", axis=axis, tiled=True)


def plain_pieces(weight, chunks):
    whole = gather_plain(weight, 1)
    rows = whole.shape[0] // (2 * chunks)
    width = whole.shape[1] // 16
    halves = []
    for half in range(2):
        pieces = []
        for chunk in range(chunks):
            start = (half * chunks + chunk) * rows
            arrays = []
            for near in range(4):
                slots = []
                for slot in range(4):
                    block = (-slot % 4) * 4 + near
                    slots.append(whole[start : start + rows, block * width : (block + 1) * width])
                arrays.append(jnp.stack(slots).reshape(2, 2, rows, width))
            pieces.append(arrays)
        halves.append(pieces)
    return halves


def vector_rows(vectors):
    rows, places, start = [], [], 0
    for vector in vectors:
        count = -(-vector.shape[0] // LANES)
        padded = jnp.pad(vector, (0, count * LANES - vector.shape[0]))
        rows.append(padded.reshape(count, LANES))
        places.append((start, count, vector.shape[0]))
        start += count
    return jnp.pad(jnp.concatenate(rows, axis=0), ((0, -start % 16), (0, 0))), places


def plain_rows(whole):
    rows = whole.shape[0] // 16
    arrays = []
    for half in range(2):
        for near in range(4):
            starts = [((-slot % 4) * 4 + near) * rows + half * rows // 2 for slot in range(4)]
            arrays.append(jnp.stack([whole[start : start + rows // 2] for start in starts]))
    return arrays


def body(
    permutes,
    wide,
    devices,
    char_ids,
    word_lengths,
    type_ids,
    cotangent,
    character_embedding_table,
    conv_weight,
    conv_bias,
    high_weight,
    high_bias,
    proj_weight,
    proj_bias,
    pos_table,
    type_table,
    embed_gain,
    embed_shift,
    qkv_weight,
    attn_bias,
    out_weight,
    out_bias,
    attn_gain,
    attn_shift,
    up_weight,
    up_bias,
    down_weight,
    down_bias,
    ffn_gain,
    ffn_shift,
):
    layers, features = high_weight.shape[:2]
    words, chars = char_ids.shape[1:]
    model_width = proj_weight.shape[1]
    conv_rows = conv_weight.shape[0]
    lengths = word_lengths[0]
    vectors = [high_bias[layer] for layer in range(layers)] + [
        attn_bias,
        type_table[0],
        type_table[1],
        proj_bias,
        embed_gain,
        embed_shift,
        out_bias,
        attn_gain,
        attn_shift,
        up_bias,
        down_bias,
        ffn_gain,
        ffn_shift,
    ]
    conv_block = jnp.pad(
        jnp.concatenate([conv_weight, conv_bias[None]], axis=0),
        ((0, LANES - conv_rows - 1), (0, 0)),
    )
    vector_block, places = vector_rows(vectors)

    if permutes:
        net = Exchange()
        window, launch = net.window, net.launch
        core_index, z, y, x = net.core, net.z, net.y, net.x
        net.load(
            "t",
            jnp.concatenate([conv_block, vector_block, pos_table.T.reshape(-1, LANES)], axis=0),
            whole=True,
        )
        chunk_rows = features // 4
        net.load("L00", high_weight[0], chunk_rows, 0)
        (
            net.state["L00"],
            net.state["t"],
            char_ids,
            lengths,
            high_weight,
            qkv_weight,
            up_weight,
        ) = lax.optimization_barrier(
            (
                net.state["L00"],
                net.state["t"],
                char_ids,
                lengths,
                high_weight,
                qkv_weight,
                up_weight,
            )
        )
        for layer, chunk in ((0, 1), (1, 0), (1, 1)):
            net.load(f"L{layer}{chunk}", high_weight[layer], chunk_rows, chunk * chunk_rows)
        encoder_splits = [
            qkv_weight.shape[1],
            out_weight.shape[0],
            proj_weight.shape[0],
        ]
        net.load(
            "e",
            jnp.concatenate(
                [qkv_weight.T, out_weight, proj_weight],
                axis=0,
            ),
        )
        net.load("up", up_weight.T)
        net.load("down", down_weight)
        net.put("L00r1", send(net.state["L00"], "z"))
        net.put("L00r3", send(net.state["L00"], "back"))
        net.move("tx", "t", "x")
        net.move("ty", "t", "y")
    else:
        window = lambda values, hold=(): values
        launch = window
        core_index = z = y = x = jnp.zeros((), jnp.int32)
    prep = sort_words(char_ids[0], lengths, chars // GROUP + 2)
    table_blocks = table_lanes(character_embedding_table)
    prep, table_blocks = window((prep, table_blocks))
    if permutes:
        net.ring_step("L00", 2)
        net.move("txy", "tx", "y")
        net.move("ex", "e", "x")
        net.move("ey", "e", "y")
        window(())
        net.ring_done("L00")
        net.state["to0"] = jnp.stack(
            [net.state["t" + part] for part in ("", "x", "y", "xy")]
        )
        net.plan_move("L00o", "x", "y")
        net.plan("to1", net.state["to0"], "z")
        launch(())
        net.turn_ring("t", 2)
        net.move("exy", "ex", "y")
        net.ring_both("L01")
        net.state["eo0"] = jnp.stack([net.state["e" + part] for part in ("", "x", "y", "xy")])
        prep, table_blocks = window((prep, table_blocks))
        net.ring_done("L01")
        net.plan_move("L01o", "x", "y")
        net.plan("to3", net.state["to2"], "z")
        prep, table_blocks = launch((prep, table_blocks))
        net.ring_both("L10")
        net.swap_chain("L00o", "L00ox", "L00oy")
    char_groups = embed_characters(prep, table_blocks)
    char_groups = window(char_groups)

    if permutes:
        net.ring_done("L10")
        conv_all, whole_vectors, pos_all = place_small(
            [net.state[f"to{step}"] for step in range(4)],
            net.place(True),
            LANES,
            [vector_block.shape[0], pos_table.size // LANES],
        )
    else:
        conv_all = gather_plain(conv_block, 1)
        whole_vectors = lax.all_gather(vector_block, "wide", axis=0, tiled=False)
        pos_all = gather_plain(pos_table.T, 0)
    filters = conv_all.shape[1]
    row = jnp.arange(LANES)[:, None]
    usable = row // CHAR_DIM < filter_widths(filters)[None, :]
    half_matrix = jnp.where(usable | (row >= conv_rows), conv_all * BF16(0.5), BF16(0.0))
    if permutes:
        net.plan("L00oxy", net.state["L00ox"], "y")
        net.plan("L01oxy", net.state["L01oy"], "x")
        net.state["eo0"] = jnp.stack([net.state["e" + part] for part in ("", "x", "y", "xy")])
        net.plan("eo1", net.state["eo0"], "z")
        half_matrix = launch(half_matrix)
        net.swap_chain("L01o", "L01ox", "L01oy")
    pooled = conv_forward(prep, char_groups, half_matrix)
    pooled, whole_vectors, pos_all = window((pooled, whole_vectors, pos_all))
    whole = [
        whole_vectors[:, start : start + count].reshape(wide, -1)[:, :size].reshape(-1)
        for start, count, size in places
    ]
    if permutes:
        net.plan_move("L10o", "x", "y")
        launch(())
        net.ring_both("L11")
        net.swap_chain("L00oxy", "L01oxy", "eo0")
        pooled, whole, pos_all = window((pooled, whole, pos_all))
        net.ring_done("L11")
        net.plan_move("L11o", "x", "y")
        net.plan("eo2", net.state["eo1"], "z")
        net.plan_swap("L10o")
        pooled = launch(pooled)
        pieces = [net.layer("L0", 2)]
    else:
        pieces = [plain_pieces(high_weight[layer], 2) for layer in range(layers)]
    high_bias_all, attn_bias_all = whole[:layers], whole[layers]
    (
        type_zero,
        type_one,
        proj_bias_all,
        gain_zero,
        shift_zero,
        out_bias_all,
        gain_one,
        shift_one,
        up_bias_all,
        down_bias_all,
        gain_two,
        shift_two,
    ) = (value.astype(F32) for value in whole[layers + 1 :])
    width = 2 * features // 16
    order = jnp.arange(8)
    near, low_slot = order // 2, order % 2
    slot_z = (z - low_slot) % 4
    place = ((slot_z & 1) * 4 + (y ^ (near >> 1)) * 2 + (x ^ (near & 1))).astype(jnp.int32)
    select = (slot_z // 2).astype(jnp.int32)
    core = core_index[None].astype(jnp.int32)
    bias_blocks = [bias.astype(F32).reshape(16, 1, width) for bias in high_bias_all]
    first_layer = highway_forward(pooled, pieces[0], bias_blocks[0], place, select, core)
    first_layer = window(first_layer)

    if permutes:
        net.plan("L10oxy", net.state["L10ox"], "y")
        net.plan("L11oxy", net.state["L11oy"], "x")
        net.plan("eo3", net.state["eo2"], "z")
        first_layer, pos_all = launch((first_layer, pos_all))
        net.swap_chain("L10ox", "L10oy", "L11o", "L11ox", "L11oy", "eo1", "eo2")
    turned = [turn(first_layer[3])]
    pos_rows = pos_all.reshape(model_width, words).T.astype(F32)
    turned, pos_rows = window((turned, pos_rows))
    if permutes:
        net.plan_swap("L10oxy", "L11oxy")
        for name in ("up", "down"):
            net.plan(name + "r1", net.state[name], "z")
            net.plan(name + "r3", net.state[name], "back")
        first_layer = net.stage(first_layer)
        for name in ("up", "down"):
            net.plan(name + "r2", net.state[name + "r1"], "z")
        net.plan_swap("eo3")
        first_layer = launch(first_layer)
        pieces.append(net.layer("L1", 2))
        qkv_all, out_all, proj_all = net.rows(
            [net.state[f"eo{step}"] for step in range(4)],
            [net.state[f"eo{step}c"] for step in range(4)],
            encoder_splits,
            True,
        )
    else:
        qkv_all, out_all, proj_all = (
            gather_plain(value, 0) for value in (qkv_weight.T, out_weight, proj_weight)
        )
    second_layer = highway_forward(first_layer[0], pieces[1], bias_blocks[1], place, select, core)
    second_layer = window(second_layer)
    if permutes:
        net.ring_done("up")
        net.ring_done("down")
        net.plan_move("upo", "x", "y")
        net.plan_move("downo", "x", "y")
        second_layer = launch(second_layer)
    states = [pooled, first_layer[0], second_layer[0]]
    transforms = [first_layer[1], second_layer[1]]
    gatings = [first_layer[2], second_layer[2]]
    perm, sorted_lengths = prep[0], prep[2]
    last = dot_tn(perm, states[2].astype(BF16)).astype(BF16)
    word_vec = dot(last, proj_all) + proj_bias_all
    type_rows = jnp.where(type_ids[0][:, None] == 1, type_one[None], type_zero[None])
    summed = word_vec + pos_rows + type_rows
    embedded = norm_rows(summed, gain_zero, shift_zero)
    turned.append(turn(second_layer[3]))
    summed, embedded, last, turned = window((summed, embedded, last, turned))

    if permutes:
        net.plan("upoxy", net.state["upox"], "y")
        net.plan("downoxy", net.state["downoy"], "x")
        embedded = launch(embedded)
        net.swap_chain("upo", "upox", "upoy", "downo")
    low_embedded = embedded.astype(BF16)
    bias_three = jnp.concatenate(
        [
            attn_bias_all[:model_width],
            jnp.zeros((model_width,), BF16),
            attn_bias_all[model_width:],
        ]
    ).astype(F32)
    qkv = (dot_nt(low_embedded, qkv_all) + bias_three).astype(BF16)
    context = attend(qkv)
    if permutes:
        context = window(context)
        net.plan_swap("downox", "downoy", "upoxy", "downoxy")
        context = launch(context)
    first_in = embedded + (dot(context, out_all) + out_bias_all)
    first = norm_rows(first_in, gain_one, shift_one)
    if permutes:
        first_in, first = window((first_in, first))
        feed_pieces = [net.near(name) + net.near(name, "c") for name in ("up", "down")]
    else:
        feed_pieces = [
            plain_rows(gather_plain(value, 0)) for value in (up_weight.T, down_weight)
        ]
    half_of = jnp.where(order % 2 == 0, 1 - core_index, core_index)
    slots = (z - (2 * half_of[:, None] + jnp.arange(2)[None, :])) % 4
    slots = slots.astype(jnp.int32)
    feed_block = (half_of * 4 + (y ^ (near >> 1)) * 2 + (x ^ (near & 1))).astype(jnp.int32)
    feed_rows = up_bias_all.shape[0] // 16
    feed_bias = jnp.moveaxis(up_bias_all.reshape(2, 2, 4, feed_rows), 1, 2).reshape(8, 1, -1)
    act, slope, hidden_out, grad_second, last_sums = feed_forward(
        first,
        feed_pieces,
        feed_bias,
        jnp.stack([down_bias_all, gain_two, shift_two]),
        cotangent[0],
        slots,
        feed_block,
        core,
    )
    grad_ffn_gain, grad_ffn_shift, grad_down_bias = last_sums[0], last_sums[1], last_sums[2]

    def sum_rows(grads, order):
        if permutes:
            return Reduction(net, *net.split(grads), order)
        return PlainReduction(grads, 0)

    def send_layer(layer, mixed, first, rows):
        sent = highway_weight_gradient(1 - core, turned[layer], mixed, first, rows, width // 2)
        key = f"layer{layer}_{first}"
        if permutes:
            net.plan(key, sent, "c")
        return layer, mixed, first, rows, (key if permutes else sent, 0)

    def keep_layer(job, order):
        layer, mixed, first, rows, (key, part) = job
        keep = highway_weight_gradient(
            core,
            turned[layer],
            mixed,
            first,
            rows,
            width // 2,
            net.state[key] if permutes else None,
            part,
        )
        if permutes:
            return Reduction(net, keep, None, order)
        other = key[:, part * rows : (part + 1) * rows]
        whole = jnp.moveaxis(jnp.concatenate([keep, other], axis=0), 1, 0).reshape(rows, -1)
        return PlainReduction([whole], 1)

    def sum_feed(keep, sent, order):
        keep, sent = (value.reshape((16,) + value.shape[3:]) for value in (keep, sent))
        if permutes:
            return Reduction(net, keep, sent, order)
        return sum_rows([jnp.concatenate([keep, sent], axis=0).reshape(-1, model_width)], "")

    def ring_of(*sums, both=False):
        return Ring(net, sums, both) if permutes else sums

    def advance(*sums):
        if permutes:
            for item in sums:
                item.step()

    def ready(*sums):
        if permutes:
            for item in sums:
                item.step(net.plan)

    def held(*sums):
        return tuple(item.key for item in sums) if permutes else ()

    def together(*sums, hold=()):
        if permutes:
            ready(*sums)
            launch(())
            window((), held(*hold))

    up_keep, up_sent, down_keep, down_sent, bias_sums, grad_resid, norm_sums = feed_forward_back(
        grad_second,
        first,
        act,
        slope,
        first_in,
        gain_one[None],
        feed_pieces,
        slots,
        feed_block,
        core,
    )
    grad_up_bias = jnp.moveaxis(bias_sums.reshape(2, 4, 2, feed_rows), 2, 1).reshape(-1)
    grad_attn_gain, grad_attn_shift, grad_out_bias = norm_sums[0], norm_sums[1], norm_sums[2]
    up_keep, up_sent, down_keep, down_sent, grad_resid = window(
        (up_keep, up_sent, down_keep, down_sent, grad_resid)
    )

    sum_up = sum_feed(up_keep, up_sent, "cxy")
    sum_down = sum_feed(down_keep, down_sent, "cyx")
    ready(sum_down, sum_up)
    grad_resid = launch(grad_resid)
    grad_branch = grad_resid.astype(BF16)
    grad_context = dot_nt(grad_branch, out_all).astype(BF16)
    grad_resid, grad_context = window((grad_resid, grad_context))
    ready(sum_down, sum_up)
    grad_context, grad_branch = launch((grad_context, grad_branch))
    grad_qkv = attend_back(qkv, grad_context)
    grad_out = dot_tn(context, grad_branch).astype(BF16)
    grad_resid, grad_qkv, grad_out = window((grad_resid, grad_qkv, grad_out))

    ready(sum_down, sum_up)
    grad_qkv, grad_resid = launch((grad_qkv, grad_resid))
    qkv_sums = column_sum(grad_qkv)
    grad_attn_bias = jnp.concatenate([qkv_sums[:model_width], qkv_sums[2 * model_width :]])
    grad_summed, grad_embed_gain, grad_embed_shift = norm_back(
        summed, gain_zero, grad_resid + dot(grad_qkv, qkv_all)
    )
    grad_word = grad_summed.astype(BF16)
    grad_proj_bias = column_sum(grad_word)
    running = dot_nt(dot(perm, grad_word).astype(BF16), proj_all)
    running = window(running)
    ring_feed = ring_of(sum_up, sum_down)
    ready(ring_feed)
    running = launch(running)
    mixed_one, sums_one, running = highway_backward(
        running, states[1], transforms[1], gatings[1], pieces[1], place, select, core
    )
    mixed_one, running, grad_qkv, grad_out, grad_word, grad_summed = window(
        (mixed_one, running, grad_qkv, grad_out, grad_word, grad_summed)
    )
    type_hot = (type_ids[0] == 1).astype(F32)[:, None]
    vector_grads = [
        grad_proj_bias,
        jnp.sum((1.0 - type_hot) * grad_summed, axis=0),
        jnp.sum(type_hot * grad_summed, axis=0),
        grad_embed_gain,
        grad_embed_shift,
        grad_attn_bias,
        grad_out_bias,
        grad_attn_gain,
        grad_attn_shift,
        grad_up_bias,
        grad_down_bias,
        grad_ffn_gain,
        grad_ffn_shift,
    ]

    half_rows, quarter = features // 2, features // 4

    def quarters(jobs, layer, mixed):
        return [
            (layer, mixed, start * quarter, quarter, (jobs[start // 2][-1][0], start % 2))
            for start in range(4)
        ]

    jobs = [send_layer(1, mixed_one, start, half_rows) for start in (0, half_rows)]
    ready(ring_feed)
    mixed_one, grad_qkv, grad_word, grad_summed = launch(
        (mixed_one, grad_qkv, grad_word, grad_summed)
    )
    grad_pos = turn(grad_summed)
    encoder_grads = [
        dot_tn(grad_qkv, low_embedded),
        grad_out,
        dot_tn(last, grad_word),
    ]
    if permutes:
        encoder_grads.append(grad_pos.reshape(-1, model_width))
        sum_encoder = sum_rows(encoder_grads, "c321xy")
        mixed_one, running, sum_encoder.terms, sum_encoder.sent = window(
            (mixed_one, running, sum_encoder.terms, sum_encoder.sent)
        )
    else:
        sum_encoder = sum_rows(encoder_grads, "")
        sum_pos = sum_rows([grad_pos], "")

    jobs = quarters(jobs, 1, mixed_one)
    one = [None] * 4
    one[0], one[2] = keep_layer(jobs[0], "yx"), keep_layer(jobs[2], "xy")
    ready(one[0], one[2], sum_encoder, ring_feed)
    running = launch(running)
    mixed_zero, sums_zero, running = highway_backward(
        running, states[0], transforms[0], gatings[0], pieces[0], place, select, core
    )
    mixed_zero, running = window((mixed_zero, running))

    one[1], one[3] = keep_layer(jobs[1], "yx"), keep_layer(jobs[3], "xy")
    jobs = [send_layer(0, mixed_zero, start, half_rows) for start in (0, half_rows)]
    grad_scaled = running * (0.5 / sorted_lengths.astype(F32))[:, None]
    ready(one[1], one[3], sum_encoder)
    grad_scaled = launch(grad_scaled)
    matrix_turned, grad_groups = conv_backward(prep, char_groups, half_matrix, grad_scaled)
    mixed_zero, matrix_turned, grad_groups = window((mixed_zero, matrix_turned, grad_groups))

    ready(*one, sum_encoder)
    mixed_zero, grad_groups = launch((mixed_zero, grad_groups))
    jobs = quarters(jobs, 0, mixed_zero)
    zero = [keep_layer(job, order_) for job, order_ in zip(jobs, ("yx", "yx", "xy", "xy"))]
    first_two = (zero[0], zero[2])
    terms = [item.terms for item in zero] if permutes else ()
    grad_table = table_gradient(prep, grad_groups, character_embedding_table.shape[0])
    first_sum, vector_places = vector_rows(vector_grads)
    last_sum, high_places = vector_rows(
        [sums_zero.reshape(-1), sums_one.reshape(-1), grad_table.reshape(-1)]
    )
    high_places = [(first_sum.shape[0] + start, *rest) for start, *rest in high_places]
    last_sum = jnp.concatenate([first_sum, last_sum], axis=0)
    terms, last_sum = window((terms, last_sum))
    last_sum = Small(net, last_sum) if permutes else lax.psum(last_sum, ("narrow", "wide"))
    for item, value in zip(zero, terms):
        item.terms = value

    if permutes:
        conv_keep, conv_sent = net.split([matrix_turned])
        net.plan("conv", conv_sent, "c")
    else:
        sum_conv = sum_rows([matrix_turned], "")
    ready(*first_two, sum_encoder, last_sum)
    launch(())
    window(())
    if permutes:
        conv_total = total_of([conv_keep, net.state["conv"]]).astype(BF16)
        conv_total = conv_total.reshape((4, 2, 2) + conv_total.shape[1:])
        zero[3].terms = [jnp.concatenate([zero[3].terms[0], conv_total], axis=3)]

    ring_one = ring_of(*one)
    together(zero[1], zero[3], *first_two, ring_one, last_sum)
    together(zero[1], zero[3], ring_one, last_sum)
    ring_first = ring_of(*first_two, both=True)
    together(ring_first, ring_one, sum_encoder, last_sum)
    ring_last = ring_of(zero[1], zero[3], both=True)
    together(ring_first, ring_last, sum_encoder, last_sum)
    together(ring_last)
    total = last_sum.result() if permutes else last_sum

    device = lax.axis_index("narrow") * wide + lax.axis_index("wide")

    def whole_vector(total, where):
        start, count, size = where
        return total[start : start + count].reshape(-1)[:size]

    def own_part(total, where):
        piece = where[2] // devices
        return lax.dynamic_slice_in_dim(whole_vector(total, where), device * piece, piece, 0)

    results = [own_part(total, where) for where in vector_places]
    (
        sum_proj_bias,
        sum_type_zero,
        sum_type_one,
        sum_embed_gain,
        sum_embed_shift,
        sum_attn_bias,
        sum_out_bias,
        sum_attn_gain,
        sum_attn_shift,
        sum_up_bias,
        sum_down_bias,
        sum_ffn_gain,
        sum_ffn_shift,
    ) = results
    sum_high_bias = jnp.stack([own_part(total, where) for where in high_places[:layers]])
    sum_table = whole_vector(total, high_places[layers]).reshape(
        character_embedding_table.shape
    )

    def rows_of(item, sizes):
        total = item.result()
        if not permutes:
            return total
        pieces, start = [], 0
        for size in sizes:
            pieces.append(total[start : start + size])
            start += size
        return pieces

    qkv_rows, sum_out, sum_proj, *rest = rows_of(
        sum_encoder,
        [
            qkv_all.shape[0] // devices,
            out_all.shape[0] // devices,
            proj_all.shape[0] // devices,
            words * model_width // devices // model_width,
        ],
    )
    if permutes:
        pos_rows = rest[0].reshape(-1, words)
    else:
        (pos_rows,) = sum_pos.result()
    if permutes:
        up_rows, down_rows = jnp.split(ring_feed.result(), 2)
    else:
        (up_rows,), (down_rows,) = sum_up.result(), sum_down.result()
    if permutes:
        first_rows, last_rows = ring_first.result(), ring_last.result()
        conv_turned = last_rows[2 * quarter :]
    else:
        (conv_turned,) = sum_conv.result()
    own_filters = lax.dynamic_slice_in_dim(
        filter_widths(filters), device * (filters // devices), filters // devices
    )
    taps = jnp.arange(conv_rows)[:, None] // CHAR_DIM
    sum_conv_weight = jnp.where(taps < own_filters[None, :], conv_turned[:, :conv_rows].T, 0.0)

    if permutes:
        parts = [first_rows[:quarter], last_rows[:quarter], first_rows[quarter:], last_rows[quarter : 2 * quarter]]
        high_rows = [jnp.concatenate(parts, axis=0), ring_one.result()]
    else:
        high_rows = [
            jnp.concatenate([part for item in sums for part in item.result()], axis=0)
            for sums in (zero, one)
        ]

    return (
        hidden_out[None],
        sum_table,
        sum_conv_weight,
        conv_turned[:, conv_rows],
        jnp.stack(high_rows),
        sum_high_bias,
        sum_proj,
        sum_proj_bias,
        pos_rows.T,
        jnp.stack([sum_type_zero, sum_type_one]),
        sum_embed_gain,
        sum_embed_shift,
        qkv_rows.T,
        sum_attn_bias,
        sum_out,
        sum_out_bias,
        sum_attn_gain,
        sum_attn_shift,
        up_rows.T,
        sum_up_bias,
        down_rows,
        sum_down_bias,
        sum_ffn_gain,
        sum_ffn_shift,
    )


def solution(mesh):
    narrow, wide = mesh.shape["narrow"], mesh.shape["wide"]
    both = ("narrow", "wide")
    placed = (
        P(both, None, None),
        P(both, None),
        P(both, None),
        P(both, None, None),
        P(),
        P(None, "wide"),
        P("wide"),
        P(None, None, "wide"),
        P(None, "wide"),
        P("wide", None),
        P("wide"),
        P(None, "wide"),
        P(None, "wide"),
        P("wide"),
        P("wide"),
        P(None, "wide"),
        P("wide"),
        P("wide", None),
        P("wide"),
        P("wide"),
        P("wide"),
        P(None, "wide"),
        P("wide"),
        P("wide", None),
        P("wide"),
        P("wide"),
        P("wide"),
    )
    return jax.shard_map(
        partial(body, (narrow, wide) == (2, 16), wide, narrow * wide),
        mesh=mesh,
        in_specs=placed,
        out_specs=(
            P(both, None, None),
            P(),
            P(None, both),
            P(both),
            P(None, None, both),
            P(None, both),
            P(both, None),
            P(both),
            P(None, both),
            P(None, both),
            P(both),
            P(both),
            P(None, both),
            P(both),
            P(both, None),
            P(both),
            P(both),
            P(both),
            P(None, both),
            P(both),
            P(both, None),
            P(both),
            P(both),
            P(both),
        ),
        check_vma=False,
    )
```

profile of v0, /device:TPU:0, one launch (start us, length us, event | category | flops | bytes accessed | tf_op | source)
XLA Modules:
  0.0 796.1 jit_solution(2272545343140954825)
XLA Ops:
  37.0 7.2 collective-permute-done.13
  47.0 10.5 %collective-permute-done.10.refs_1_ = bf16[4,352,128]{2,1,0:T(8,128)(2,1)S(1)} collective-permute-done((bf16[4,352,128]{2,1,0:T(8,128)(2,1)S(1)}, bf16[4,352,128]{2,1,0:T(8,128)(2,1)S(1)}, u32[]{:S(2)}, u32[]{:S(2)}) %collective-permute-start.10) | collective-permute-done | bytes 360480 | tf_op jit(solution)/shard_map/ppermute | solution.py:634
  57.5 5.6 collective-permute-done.15
  63.6 5.9 collective-permute-done.12
  74.1 7.8 collective-permute-done.19
  81.9 6.7 collective-permute-done.20
  89.4 8.2 %collective-permute-done.21 = bf16[512,256]{1,0:T(8,128)(2,1)S(1)} collective-permute-done((bf16[512,256]{1,0:T(8,128)(2,1)}, bf16[512,256]{1,0:T(8,128)(2,1)S(1)}, u32[]{:S(2)}, u32[]{:S(2)}) %collective-permute-start.21) | collective-permute-done | bytes 262176 | tf_op jit(solution)/shard_map/ppermute | solution.py:634
  97.7 4.9 embed.1.g_ref
  115.5 12.2 %conv_forward.1.h_ref = f32[512,2048]{1,0:T(8,128)S(1)} custom-call(s32[8]{0:T(128)S(1)} %pad_add_fusion.scalar_ref, s32[816]{0:T(1024)S(1)} %fusion.76.tile_ref, s32[816]{0:T(1024)S(1)} %subtract_select_fusion.pos_ref, bf16[8,512,128]{2,1,0:T(8,128)(2,1)S(1)} %copy-done.57, bf16[128,2048]{1,0:T(8,128)(2,1)S(1)} %or_select_fusion.w_ref, ...), custom_call_target="tpu_custom_call" | custom-call | flops 17600000000 | bytes 48000000 | tf_op jit(solution)/shard_map/conv_forward/pallas_call | solution.py:175
  129.8 11.0 %collective-permute-done.32.refs_1_ = bf16[4,160,768]{2,1,0:T(8,128)(2,1)S(1)} collective-permute-done((bf16[4,160,768]{2,1,0:T(8,128)(2,1)S(1)}, bf16[4,160,768]{2,1,0:T(8,128)(2,1)S(1)}, u32[]{:S(2)}, u32[]{:S(2)}) %collective-permute-start.32) | collective-permute-done | bytes 983072 | tf_op jit(solution)/shard_map/ppermute | solution.py:634
  153.3 7.4 collective-permute-done.27
  181.1 19.5 %highway_forward.2 = (f32[512,2048]{1,0:T(8,128)}, f32[512,2048]{1,0:T(8,128)}, f32[512,2048]{1,0:T(8,128)}, bf16[512,2048]{1,0:T(8,128)(2,1)}) custom-call(s32[8]{0:T(128)} %get-tuple-element.1014.place_ref, s32[8]{0:T(128)} %get-tuple-element.1013.select_ref, s32[1]{0:T(128)} %bitcast.core_ref.which_ref, f32[512,2048]{1,0:T(8,128)} %copy-done.59, ...), custom_call_target="tpu_custom_call" | custom-call | flops 20899999744 | bytes 57000000 | tf_op jit(solution)/shard_map/highway_forward/pallas_call | solution.py:385
  200.6 4.7 collective-permute-done.41.refs_2_
  223.6 15.1 %collective-permute-done.45.refs_3_ = bf16[4,160,768]{2,1,0:T(8,128)(2,1)} collective-permute-done((bf16[4,160,768]{2,1,0:T(8,128)(2,1)}, bf16[4,160,768]{2,1,0:T(8,128)(2,1)}, u32[]{:S(2)}, u32[]{:S(2)}) %collective-permute-start.45) | collective-permute-done | bytes 983072 | tf_op jit(solution)/shard_map/ppermute | solution.py:634
  257.8 19.4 %highway_forward.3 = (f32[512,2048]{1,0:T(8,128)}, f32[512,2048]{1,0:T(8,128)}, f32[512,2048]{1,0:T(8,128)}, bf16[512,2048]{1,0:T(8,128)(2,1)}) custom-call(s32[8]{0:T(128)} %get-tuple-element.1014.place_ref, s32[8]{0:T(128)} %get-tuple-element.1013.select_ref, s32[1]{0:T(128)} %bitcast.core_ref.which_ref, f32[512,2048]{1,0:T(8,128)} %get-tuple-element.590.h_ref, ...), custom_call_target="tpu_custom_call" | custom-call | flops 20899999744 | bytes 57000000 | tf_op jit(solution)/shard_map/highway_forward/pallas_call | solution.py:385
  286.6 8.4 %place_rows.1 = (bf16[2304,768]{1,0:T(8,128)(2,1)S(1)}, bf16[768,768]{1,0:T(8,128)(2,1)S(1)}, bf16[2048,768]{1,0:T(8,128)(2,1)S(1)}) custom-call(s32[16]{0:T(128)S(1)} %fusion.80.place_ref, s32[1]{0:T(128)} %bitcast.core_ref.which_ref, bf16[4,160,768]{2,1,0:T(8,128)(2,1)S(1)} %pad_maximum_fusion.8.refs_0_, bf16[4,160,768]{2,1,0:T(8,128)(2,1)S(1)} %copy-done.37, ...), custom_call_target="tpu_custom_call" | custom-call | flops 7699999744 | bytes 21000000 | tf_op jit(solution)/shard_map/place_rows/pallas_call | solution.py:560
  314.4 4.6 fusion.query_ref.key_ref.value_ref
  319.2 11.1 %attend.1 = bf16[512,768]{1,0:T(8,128)(2,1)S(1)} custom-call(bf16[512,2304]{1,0:T(8,128)(2,1)S(1)} %fusion.query_ref.key_ref.value_ref, bf16[512,2304]{1,0:T(8,128)(2,1)S(1)} %fusion.query_ref.key_ref.value_ref, bf16[512,2304]{1,0:T(8,128)(2,1)S(1)} %fusion.query_ref.key_ref.value_ref), custom_call_target="tpu_custom_call" | custom-call | flops 13200000000 | bytes 36000000 | tf_op jit(solution)/shard_map/attend/pallas_call | solution.py:1240
  336.1 21.3 %feed_forward.1 = (bf16[8,512,384]{2,1,0:T(8,128)(2,1)}, bf16[8,512,384]{2,1,0:T(8,128)(2,1)}, bf16[512,768]{1,0:T(8,128)(2,1)}, f32[512,768]{1,0:T(8,128)}, f32[8,768]{1,0:T(8,128)}) custom-call(s32[8,2]{1,0:T(8,128)} %add_select_fusion.slot_ref, s32[8]{0:T(128)} %add_add_fusion.2.block_ref, s32[1]{0:T(128)} %bitcast.core_ref.which_ref, ...), custom_call_target="tpu_custom_call" | custom-call | flops 22000001024 | bytes 60000000 | tf_op jit(solution)/shard_map/feed_forward/pallas_call | solution.py:1044
  357.4 24.3 %feed_back.1 = (bf16[2,4,2,96,768]{4,3,2,1,0:T(8,128)(2,1)}, bf16[2,4,2,96,768]{4,3,2,1,0:T(8,128)(2,1)}, bf16[2,4,2,96,768]{4,3,2,1,0:T(8,128)(2,1)}, bf16[2,4,...) custom-call(s32[8,2]{1,0:T(8,128)} %add_select_fusion.slot_ref, ...), custom_call_target="tpu_custom_call" | custom-call | flops 27499999232 | bytes 75000000 | tf_op jit(solution)/shard_map/feed_back/pallas_call | solution.py:1170
  394.6 16.6 %attend_back.1 = (bf16[512,768]{1,0:T(8,128)(2,1)S(1)}, bf16[512,768]{1,0:T(8,128)(2,1)S(1)}, bf16[512,768]{1,0:T(8,128)(2,1)S(1)}) custom-call(bf16[512,2304]{1,0:T(8,128)(2,1)S(1)} %copy-done.55, bf16[512,2304]{1,0:T(8,128)(2,1)S(1)} %copy-done.55, bf16[512,2304]{1,0:T(8,128)(2,1)S(1)} %copy-done.55, bf16[512,768]{1,0:T(8,128)(2,1)S(1)} %convolution_convert_fusion.4.grad_ref), custom_call_target="tpu_custom_call" | custom-call | flops 18699999232 | bytes 51000000 | tf_op jit(solution)/shard_map/attend_back/pallas_call | solution.py:1275
  413.3 8.5 %collective-permute-done.78 = bf16[4,2,96,768]{3,2,1,0:T(8,128)(2,1)S(1)} collective-permute-done((bf16[4,2,96,768]{3,2,1,0:T(8,128)(2,1)S(1)}, bf16[4,2,96,768]{3,2,1,0:T(8,128)(2,1)S(1)}, u32[]{:S(2)}, u32[]{:S(2)}) %collective-permute-start.78) | collective-permute-done | bytes 1179680 | tf_op jit(solution)/shard_map/ppermute | solution.py:634
  432.8 6.6 fusion.26.grad_ref
  448.4 21.2 %highway_backward.2 = (bf16[2,512,2048]{2,1,0:T(8,128)(2,1)}, f32[2,1,2048]{2,1,0:T(1,128)}, f32[512,2048]{1,0:T(8,128)}) custom-call(s32[8]{0:T(128)} %get-tuple-element.1014.place_ref, s32[8]{0:T(128)} %get-tuple-element.1013.select_ref, s32[1]{0:T(128)} %bitcast.core_ref.which_ref, f32[512,2048]{1,0:T(8,128)} %fusion.26.grad_ref, ...), custom_call_target="tpu_custom_call" | custom-call | flops 23100000256 | bytes 63000000 | tf_op jit(solution)/shard_map/highway_backward/pallas_call | solution.py:449
  521.4 21.5 %highway_backward.3 = (bf16[2,512,2048]{2,1,0:T(8,128)(2,1)}, f32[2,1,2048]{2,1,0:T(1,128)}, f32[512,2048]{1,0:T(8,128)}) custom-call(s32[8]{0:T(128)} %get-tuple-element.1014.place_ref, s32[8]{0:T(128)} %get-tuple-element.1013.select_ref, s32[1]{0:T(128)} %bitcast.core_ref.which_ref, f32[512,2048]{1,0:T(8,128)} %get-tuple-element.745.grad_ref, ...), custom_call_target="tpu_custom_call" | custom-call | flops 23100000256 | bytes 63000000 | tf_op jit(solution)/shard_map/highway_backward/pallas_call | solution.py:449
  573.8 34.5 %conv_backward.1 = (bf16[2048,128]{1,0:T(8,128)(2,1)S(1)}, f32[8,512,128]{2,1,0:T(8,128)S(1)}) custom-call(s32[8]{0:T(128)S(1)} %copy-done.47, s32[816]{0:T(1024)S(1)} %copy-done.32, s32[816]{0:T(1024)S(1)} %copy-done.34, bf16[8,512,128]{2,1,0:T(8,128)(2,1)S(1)} %copy-done.58, bf16[128,2048]{1,0:T(8,128)(2,1)S(1)} %copy-done.26, s32[512,1]{1,0:T(8,128)S(1)} %copy-done.30, ...), custom_call_target="tpu_custom_call" | custom-call | flops 38499999744 | bytes 105000000 | tf_op jit(solution)/shard_map/conv_backward/pallas_call | solution.py:232
  666.5 7.6 collective-permute-done.101
  683.7 9.4 %collective-permute-done.110 = f32[224,128]{1,0:T(8,128)S(1)} collective-permute-done((f32[224,128]{1,0:T(8,128)S(1)}, f32[224,128]{1,0:T(8,128)S(1)}, u32[]{:S(2)}, u32[]{:S(2)}) %collective-permute-start.110) | collective-permute-done | bytes 114720 | tf_op jit(solution)/shard_map/ppermute | solution.py:634
  696.5 18.6 %collective-permute-done.107 = bf16[4,512,128]{2,1,0:T(8,128)(2,1)} collective-permute-done((bf16[4,512,128]{2,1,0:T(8,128)(2,1)}, bf16[4,512,128]{2,1,0:T(8,128)(2,1)}, u32[]{:S(2)}, u32[]{:S(2)}) %collective-permute-start.107) | collective-permute-done | bytes 524320 | tf_op jit(solution)/shard_map/ppermute | solution.py:634
  744.6 5.7 collective-permute-done.116
  750.3 5.6 collective-permute-done.117
  763.3 15.3 %collective-permute-done.124 = f32[224,128]{1,0:T(8,128)S(1)} collective-permute-done((f32[224,128]{1,0:T(8,128)S(1)}, f32[224,128]{1,0:T(8,128)S(1)}, u32[]{:S(2)}, u32[]{:S(2)}) %collective-permute-start.124) | collective-permute-done | bytes 114720 | tf_op jit(solution)/shard_map/ppermute | solution.py:634
  (908 shorter events, 404.1 us)
Async XLA Ops:
  29.9 40.0 %collective-permute-start.22 = (bf16[4,512,256]{2,1,0:T(8,128)(2,1)S(1)}, bf16[4,512,256]{2,1,0:T(8,128)(2,1)S(1)}, u32[]{:S(2)}, u32[]{:S(2)}) collective-permute-start(bf16[4,512,256]{2,1,0:T(8,128)(2,1)S(1)} %pad_maximum_fusion.4), channel_id=1, source_target_pairs={{0,16},{16,0},{1,17},{17,1},{2,18},{18,2},{3,19},{19,3},{4,20},{20... | collective-permute-start | bytes 3145736 | tf_op jit(solution)/shard_map/ppermute | solution.py:633
  30.0 39.8 %collective-permute-start.8 = (bf16[4,512,256]{2,1,0:T(8,128)(2,1)S(1)}, bf16[4,512,256]{2,1,0:T(8,128)(2,1)S(1)}, u32[]{:S(2)}, u32[]{:S(2)}) collective-permute-start(bf16[4,512,256]{2,1,0:T(8,128)(2,1)S(1)} %pad_maximum_fusion.4), channel_id=1, source_target_pairs={{0,1},{1,0},{2,3},{3,2},{4,5},{5,4},{6,7},{7,6},{8,9},{9,8},{10,11... | collective-permute-start | bytes 3145736 | tf_op jit(solution)/shard_map/ppermute | solution.py:634
  31.6 38.3 %collective-permute-start.9 = (bf16[4,512,256]{2,1,0:T(8,128)(2,1)S(1)}, bf16[4,512,256]{2,1,0:T(8,128)(2,1)}, u32[]{:S(2)}, u32[]{:S(2)}) collective-permute-start(bf16[4,512,256]{2,1,0:T(8,128)(2,1)S(1)} %pad_maximum_fusion.4), channel_id=1, source_target_pairs={{0,2},{1,3},{2,0},{3,1},{4,6},{5,7},{6,4},{7,5},{8,10},{9,11},{10,... | collective-permute-start | bytes 3145736 | tf_op jit(solution)/shard_map/ppermute | solution.py:634
  72.5 35.1 %collective-permute-start.16 = (bf16[4,512,256]{2,1,0:T(8,128)(2,1)}, bf16[4,512,256]{2,1,0:T(8,128)(2,1)}, u32[]{:S(2)}, u32[]{:S(2)}) collective-permute-start(bf16[4,512,256]{2,1,0:T(8,128)(2,1)} %pad_maximum_fusion.5), channel_id=1, source_target_pairs={{0,1},{1,0},{2,3},{3,2},{4,5},{5,4},{6,7},{7,6},{8,9},{9,8},{10,11... | collective-permute-start | bytes 3145736 | tf_op jit(solution)/shard_map/ppermute | solution.py:634
  73.0 34.6 %collective-permute-start.17 = (bf16[4,512,256]{2,1,0:T(8,128)(2,1)}, bf16[4,512,256]{2,1,0:T(8,128)(2,1)}, u32[]{:S(2)}, u32[]{:S(2)}) collective-permute-start(bf16[4,512,256]{2,1,0:T(8,128)(2,1)} %pad_maximum_fusion.5), channel_id=1, source_target_pairs={{0,2},{1,3},{2,0},{3,1},{4,6},{5,7},{6,4},{7,5},{8,10},{9,11},{10,... | collective-permute-start | bytes 3145736 | tf_op jit(solution)/shard_map/ppermute | solution.py:634
  73.5 34.1 %collective-permute-start.24 = (bf16[4,512,256]{2,1,0:T(8,128)(2,1)}, bf16[4,512,256]{2,1,0:T(8,128)(2,1)}, u32[]{:S(2)}, u32[]{:S(2)}) collective-permute-start(bf16[4,512,256]{2,1,0:T(8,128)(2,1)} %collective-permute-done.9), channel_id=1, source_target_pairs={{0,16},{16,0},{1,17},{17,1},{2,18},{18,2},{3,19},{19,3},{4,20},{20... | collective-permute-start | bytes 3145736 | tf_op jit(solution)/shard_map/ppermute | solution.py:633
  73.6 34.1 %collective-permute-start.33 = (bf16[4,512,256]{2,1,0:T(8,128)(2,1)}, bf16[4,512,256]{2,1,0:T(8,128)(2,1)}, u32[]{:S(2)}, u32[]{:S(2)}) collective-permute-start(bf16[4,512,256]{2,1,0:T(8,128)(2,1)} %pad_maximum_fusion.5), channel_id=1, source_target_pairs={{0,16},{16,0},{1,17},{17,1},{2,18},{18,2},{3,19},{19,3},{4,20},{20... | collective-permute-start | bytes 3145736 | tf_op jit(solution)/shard_map/ppermute | solution.py:633
  114.4 26.5 %collective-permute-start.30 = (bf16[4,512,256]{2,1,0:T(8,128)(2,1)S(1)}, bf16[4,512,256]{2,1,0:T(8,128)(2,1)S(1)}, u32[]{:S(2)}, u32[]{:S(2)}) collective-permute-start(bf16[4,512,256]{2,1,0:T(8,128)(2,1)S(1)} %copy-done.161), channel_id=1, source_target_pairs={{0,2},{1,3},{2,0},{3,1},{4,6},{5,7},{6,4},{7,5},{8,10},{9,11},{10,... | collective-permute-start | bytes 3145736 | tf_op jit(solution)/shard_map/ppermute | solution.py:634
  114.9 25.9 %collective-permute-start.31 = (bf16[4,512,256]{2,1,0:T(8,128)(2,1)}, bf16[4,512,256]{2,1,0:T(8,128)(2,1)S(1)}, u32[]{:S(2)}, u32[]{:S(2)}) collective-permute-start(bf16[4,512,256]{2,1,0:T(8,128)(2,1)} %collective-permute-done.17), channel_id=1, source_target_pairs={{0,1},{1,0},{2,3},{3,2},{4,5},{5,4},{6,7},{7,6},{8,9},{9,8},{10,11... | collective-permute-start | bytes 3145736 | tf_op jit(solution)/shard_map/ppermute | solution.py:634
  177.8 27.5 %collective-permute-start.39 = (bf16[4,512,256]{2,1,0:T(8,128)(2,1)S(1)}, bf16[4,512,256]{2,1,0:T(8,128)(2,1)S(1)}, u32[]{:S(2)}, u32[]{:S(2)}) collective-permute-start(bf16[4,512,256]{2,1,0:T(8,128)(2,1)S(1)} %pad_maximum_fusion.7), channel_id=1, source_target_pairs={{0,1},{1,0},{2,3},{3,2},{4,5},{5,4},{6,7},{7,6},{8,9},{9,8},{10,11... | collective-permute-start | bytes 3145736 | tf_op jit(solution)/shard_map/ppermute | solution.py:634
  178.4 26.9 %collective-permute-start.40 = (bf16[4,512,256]{2,1,0:T(8,128)(2,1)S(1)}, bf16[4,512,256]{2,1,0:T(8,128)(2,1)}, u32[]{:S(2)}, u32[]{:S(2)}) collective-permute-start(bf16[4,512,256]{2,1,0:T(8,128)(2,1)S(1)} %pad_maximum_fusion.7), channel_id=1, source_target_pairs={{0,2},{1,3},{2,0},{3,1},{4,6},{5,7},{6,4},{7,5},{8,10},{9,11},{10,... | collective-permute-start | bytes 3145736 | tf_op jit(solution)/shard_map/ppermute | solution.py:634
  211.1 27.6 %collective-permute-start.43 = (bf16[4,512,256]{2,1,0:T(8,128)(2,1)}, bf16[4,512,256]{2,1,0:T(8,128)(2,1)}, u32[]{:S(2)}, u32[]{:S(2)}) collective-permute-start(bf16[4,512,256]{2,1,0:T(8,128)(2,1)} %collective-permute-done.25), channel_id=1, source_target_pairs={{0,2},{1,3},{2,0},{3,1},{4,6},{5,7},{6,4},{7,5},{8,10},{9,11},{10,... | collective-permute-start | bytes 3145736 | tf_op jit(solution)/shard_map/ppermute | solution.py:634
  211.6 27.1 %collective-permute-start.44 = (bf16[4,512,256]{2,1,0:T(8,128)(2,1)}, bf16[4,512,256]{2,1,0:T(8,128)(2,1)}, u32[]{:S(2)}, u32[]{:S(2)}) collective-permute-start(bf16[4,512,256]{2,1,0:T(8,128)(2,1)} %collective-permute-done.40), channel_id=1, source_target_pairs={{0,1},{1,0},{2,3},{3,2},{4,5},{5,4},{6,7},{7,6},{8,9},{9,8},{10,11... | collective-permute-start | bytes 3145736 | tf_op jit(solution)/shard_map/ppermute | solution.py:634
  278.3 28.9 %collective-permute-start.68 = (bf16[4,96,768]{2,1,0:T(8,128)(2,1)S(1)}, bf16[4,96,768]{2,1,0:T(8,128)(2,1)S(1)}, u32[]{:S(2)}, u32[]{:S(2)}) collective-permute-start(bf16[4,96,768]{2,1,0:T(8,128)(2,1)S(1)} %pad_maximum_fusion.9.refs_0_), channel_id=1, source_target_pairs={{0,16},{16,0},{1,17},{17,1},{2,18},{18,2},{3,19},{19,3},{4,20},{20... | collective-permute-start | bytes 1769480 | tf_op jit(solution)/shard_map/ppermute | solution.py:633
  279.0 26.7 %collective-permute-start.62 = (bf16[4,96,768]{2,1,0:T(8,128)(2,1)S(1)}, bf16[4,96,768]{2,1,0:T(8,128)(2,1)S(1)}, u32[]{:S(2)}, u32[]{:S(2)}) collective-permute-start(bf16[4,96,768]{2,1,0:T(8,128)(2,1)S(1)} %pad_maximum_fusion.9.refs_0_), channel_id=1, source_target_pairs={{0,1},{1,0},{2,3},{3,2},{4,5},{5,4},{6,7},{7,6},{8,9},{9,8},{10,11... | collective-permute-start | bytes 1769480 | tf_op jit(solution)/shard_map/ppermute | solution.py:634
  279.6 26.1 %collective-permute-start.63 = (bf16[4,96,768]{2,1,0:T(8,128)(2,1)S(1)}, bf16[4,96,768]{2,1,0:T(8,128)(2,1)}, u32[]{:S(2)}, u32[]{:S(2)}) collective-permute-start(bf16[4,96,768]{2,1,0:T(8,128)(2,1)S(1)} %pad_maximum_fusion.9.refs_0_), channel_id=1, source_target_pairs={{0,2},{1,3},{2,0},{3,1},{4,6},{5,7},{6,4},{7,5},{8,10},{9,11},{10,... | collective-permute-start | bytes 1769480 | tf_op jit(solution)/shard_map/ppermute | solution.py:634
  281.0 25.9 %collective-permute-start.64 = (bf16[4,96,768]{2,1,0:T(8,128)(2,1)S(1)}, bf16[4,96,768]{2,1,0:T(8,128)(2,1)S(1)}, u32[]{:S(2)}, u32[]{:S(2)}) collective-permute-start(bf16[4,96,768]{2,1,0:T(8,128)(2,1)S(1)} %pad_maximum_fusion.10.refs_8_), channel_id=1, source_target_pairs={{0,1},{1,0},{2,3},{3,2},{4,5},{5,4},{6,7},{7,6},{8,9},{9,8},{10,11... | collective-permute-start | bytes 1769480 | tf_op jit(solution)/shard_map/ppermute | solution.py:634
  393.5 28.3 %collective-permute-start.78 = (bf16[4,2,96,768]{3,2,1,0:T(8,128)(2,1)S(1)}, bf16[4,2,96,768]{3,2,1,0:T(8,128)(2,1)S(1)}, u32[]{:S(2)}, u32[]{:S(2)}) collective-permute-start(bf16[4,2,96,768]{3,2,1,0:T(8,128)(2,1)S(1)} %fusion.6), channel_id=1, source_target_pairs={{0,2},{1,3},{2,0},{3,1},{4,6},{5,7},{6,4},{7,5},{8,10},{9,11},{10,... | collective-permute-start | bytes 3538952 | tf_op jit(solution)/shard_map/ppermute | solution.py:634
  394.1 28.0 %collective-permute-start.79 = (bf16[4,2,96,768]{3,2,1,0:T(8,128)(2,1)S(1)}, bf16[4,2,96,768]{3,2,1,0:T(8,128)(2,1)S(1)}, u32[]{:S(2)}, u32[]{:S(2)}) collective-permute-start(bf16[4,2,96,768]{3,2,1,0:T(8,128)(2,1)S(1)} %fusion.7), channel_id=1, source_target_pairs={{0,1},{1,0},{2,3},{3,2},{4,5},{5,4},{6,7},{7,6},{8,9},{9,8},{10,11... | collective-permute-start | bytes 3538952 | tf_op jit(solution)/shard_map/ppermute | solution.py:634
  514.1 38.9 %collective-permute-start.88 = (bf16[16,176,768]{2,1,0:T(8,128)(2,1)}, bf16[16,176,768]{2,1,0:T(8,128)(2,1)}, u32[]{:S(2)}, u32[]{:S(2)}) collective-permute-start(bf16[16,176,768]{2,1,0:T(8,128)(2,1)} %pad_maximum_fusion.1), channel_id=1, source_target_pairs={{0,16},{16,0},{1,17},{17,1},{2,18},{18,2},{3,19},{19,3},{4,20},{20... | collective-permute-start | bytes 12976136 | tf_op jit(solution)/shard_map/ppermute | solution.py:633
  518.3 34.7 %collective-permute-start.86 = (bf16[4,2,512,128]{3,2,1,0:T(8,128)(2,1)}, bf16[4,2,512,128]{3,2,1,0:T(8,128)(2,1)}, u32[]{:S(2)}, u32[]{:S(2)}) collective-permute-start(bf16[4,2,512,128]{3,2,1,0:T(8,128)(2,1)} %dynamic-slice_bitcast_fusion.8), channel_id=1, source_target_pairs={{0,2},{1,3},{2,0},{3,1},{4,6},{5,7},{6,4},{7,5},{8,10},{9,11},{10,... | collective-permute-start | bytes 3145736 | tf_op jit(solution)/shard_map/ppermute | solution.py:634
  519.7 33.3 %collective-permute-start.87 = (bf16[4,2,512,128]{3,2,1,0:T(8,128)(2,1)S(1)}, bf16[4,2,512,128]{3,2,1,0:T(8,128)(2,1)}, u32[]{:S(2)}, u32[]{:S(2)}) collective-permute-start(bf16[4,2,512,128]{3,2,1,0:T(8,128)(2,1)S(1)} %copy-done.84), channel_id=1, source_target_pairs={{0,1},{1,0},{2,3},{3,2},{4,5},{5,4},{6,7},{7,6},{8,9},{9,8},{10,11... | collective-permute-start | bytes 3145736 | tf_op jit(solution)/shard_map/ppermute | solution.py:634
  521.2 31.8 %collective-permute-start.89 = (bf16[192,768]{1,0:T(8,128)(2,1)}, bf16[192,768]{1,0:T(8,128)(2,1)S(1)}, u32[]{:S(2)}, u32[]{:S(2)}) collective-permute-start(bf16[192,768]{1,0:T(8,128)(2,1)} %fusion.30), channel_id=1, source_target_pairs={{0,4},{1,5},{2,6},{3,7},{4,8},{5,9},{6,10},{7,11},{8,12},{9,13},{1... | collective-permute-start | bytes 884744 | tf_op jit(solution)/shard_map/ppermute | solution.py:634
  567.8 44.0 %collective-permute-start.90 = (bf16[16,1024,128]{2,1,0:T(8,128)(2,1)}, bf16[16,1024,128]{2,1,0:T(8,128)(2,1)}, u32[]{:S(2)}, u32[]{:S(2)}) collective-permute-start(bf16[16,1024,128]{2,1,0:T(8,128)(2,1)} %highway_weight.17), channel_id=1, source_target_pairs={{0,16},{16,0},{1,17},{17,1},{2,18},{18,2},{3,19},{19,3},{4,20},{20... | collective-permute-start | bytes 12582920 | tf_op jit(solution)/shard_map/ppermute | solution.py:633
  567.8 44.0 %collective-permute-start.91 = (bf16[16,1024,128]{2,1,0:T(8,128)(2,1)}, bf16[16,1024,128]{2,1,0:T(8,128)(2,1)}, u32[]{:S(2)}, u32[]{:S(2)}) collective-permute-start(bf16[16,1024,128]{2,1,0:T(8,128)(2,1)} %highway_weight.18), channel_id=1, source_target_pairs={{0,16},{16,0},{1,17},{17,1},{2,18},{18,2},{3,19},{19,3},{4,20},{20... | collective-permute-start | bytes 12582920 | tf_op jit(solution)/shard_map/ppermute | solution.py:633
  569.3 42.5 %collective-permute-start.92 = (bf16[4,2,512,128]{3,2,1,0:T(8,128)(2,1)}, bf16[4,2,512,128]{3,2,1,0:T(8,128)(2,1)S(1)}, u32[]{:S(2)}, u32[]{:S(2)}) collective-permute-start(bf16[4,2,512,128]{3,2,1,0:T(8,128)(2,1)} %dynamic-slice_bitcast_fusion.6), channel_id=1, source_target_pairs={{0,2},{1,3},{2,0},{3,1},{4,6},{5,7},{6,4},{7,5},{8,10},{9,11},{10,... | collective-permute-start | bytes 3145736 | tf_op jit(solution)/shard_map/ppermute | solution.py:634
  570.1 41.8 %collective-permute-start.93 = (bf16[4,2,512,128]{3,2,1,0:T(8,128)(2,1)}, bf16[4,2,512,128]{3,2,1,0:T(8,128)(2,1)S(1)}, u32[]{:S(2)}, u32[]{:S(2)}) collective-permute-start(bf16[4,2,512,128]{3,2,1,0:T(8,128)(2,1)} %dynamic-slice_bitcast_fusion.5), channel_id=1, source_target_pairs={{0,1},{1,0},{2,3},{3,2},{4,5},{5,4},{6,7},{7,6},{8,9},{9,8},{10,11... | collective-permute-start | bytes 3145736 | tf_op jit(solution)/shard_map/ppermute | solution.py:634
  570.6 41.2 %collective-permute-start.94 = (bf16[2,2,176,768]{3,2,1,0:T(8,128)(2,1)}, bf16[2,2,176,768]{3,2,1,0:T(8,128)(2,1)S(1)}, u32[]{:S(2)}, u32[]{:S(2)}) collective-permute-start(bf16[2,2,176,768]{3,2,1,0:T(8,128)(2,1)} %fusion.11), channel_id=1, source_target_pairs={{0,4},{1,5},{2,6},{3,7},{4,8},{5,9},{6,10},{7,11},{8,12},{9,13},{1... | collective-permute-start | bytes 3244040 | tf_op jit(solution)/shard_map/ppermute | solution.py:634
  679.4 35.8 %collective-permute-start.106 = (bf16[4,2,576,128]{3,2,1,0:T(8,128)(2,1)}, bf16[4,2,576,128]{3,2,1,0:T(8,128)(2,1)}, u32[]{:S(2)}, u32[]{:S(2)}) collective-permute-start(bf16[4,2,576,128]{3,2,1,0:T(8,128)(2,1)} %fusion.5), channel_id=1, source_target_pairs={{0,1},{1,0},{2,3},{3,2},{4,5},{5,4},{6,7},{7,6},{8,9},{9,8},{10,11... | collective-permute-start | bytes 3538952 | tf_op jit(solution)/shard_map/ppermute | solution.py:634
  681.3 33.9 %collective-permute-start.105 = (bf16[4,2,512,128]{3,2,1,0:T(8,128)(2,1)}, bf16[4,2,512,128]{3,2,1,0:T(8,128)(2,1)}, u32[]{:S(2)}, u32[]{:S(2)}) collective-permute-start(bf16[4,2,512,128]{3,2,1,0:T(8,128)(2,1)} %dynamic-slice_bitcast_fusion.2), channel_id=1, source_target_pairs={{0,2},{1,3},{2,0},{3,1},{4,6},{5,7},{6,4},{7,5},{8,10},{9,11},{10,... | collective-permute-start | bytes 3145736 | tf_op jit(solution)/shard_map/ppermute | solution.py:634
  683.1 32.1 %collective-permute-start.107 = (bf16[4,512,128]{2,1,0:T(8,128)(2,1)}, bf16[4,512,128]{2,1,0:T(8,128)(2,1)}, u32[]{:S(2)}, u32[]{:S(2)}) collective-permute-start(bf16[4,512,128]{2,1,0:T(8,128)(2,1)} %fusion.18), channel_id=1, source_target_pairs={{0,1},{1,0},{2,3},{3,2},{4,5},{5,4},{6,7},{7,6},{8,9},{9,8},{10,11... | collective-permute-start | bytes 1572872 | tf_op jit(solution)/shard_map/ppermute | solution.py:634
  683.7 31.5 %collective-permute-start.108 = (bf16[4,512,128]{2,1,0:T(8,128)(2,1)}, bf16[4,512,128]{2,1,0:T(8,128)(2,1)}, u32[]{:S(2)}, u32[]{:S(2)}) collective-permute-start(bf16[4,512,128]{2,1,0:T(8,128)(2,1)} %fusion.17), channel_id=1, source_target_pairs={{0,2},{1,3},{2,0},{3,1},{4,6},{5,7},{6,4},{7,5},{8,10},{9,11},{10,... | collective-permute-start | bytes 1572872 | tf_op jit(solution)/shard_map/ppermute | solution.py:634
  (284 other events, 3643.2 us)
where the time goes:
time: 809 us; the launch traced here: 796 us
  Pallas kernels  265 us (33%)
  waiting for transfers between devices  216 us (27%)
  other arithmetic  105 us (13%)
  starting transfers between devices  96.1 us (12%)
  local copies, waits for them, and re-layouts  80.9 us (10%)
  matrix products  28.2 us (3%)
    ppermute x89, waiting for transfers between devices, send(): return lax.ppermute(value, 'wide', LINKS[link])  202 us
    ppermute x89, starting transfers between devices, send(): return lax.ppermute(value, 'wide', LINKS[link])  89.2 us
    pallas_call x2, Pallas kernels, highway_backward(): pl.pallas_call(partial(highway_backward_kernel, layout), grid_spec=pltpu....  42.7 us
    pallas_call x12, Pallas kernels, highway_weight_gradient(): pl.pallas_call(weight_kernel, grid_spec=pltpu.PrefetchScalarGridSpec(num_...  40.9 us
    pallas_call x2, Pallas kernels, highway_forward(): pl.pallas_call(partial(highway_forward_kernel, layout), grid_spec=pltpu.P...  38.9 us
    unnamed x400, local copies, waits for them, and re-layouts  37.8 us
    pallas_call x1, Pallas kernels, conv_backward(): pl.pallas_call(conv_backward_kernel, out_shape=(jax.ShapeDtypeStruct((fil...  34.5 us
    pallas_call x1, Pallas kernels, feed_forward_back(): pl.pallas_call(partial(feed_forward_back_kernel, len(up)), grid_spec=pltp...  24.3 us
  transfers between devices with their start and end apart: 126, of which 50 were waited for; matrix products, arithmetic and copies ran while one was open for 16% of the time, Pallas kernels for 25%

commit v1 on v0

--- a/solution.py
+++ b/solution.py
@@ -1004,7 +1004,7 @@
 
     join_rows(slot_ref, core_ref[0], refs[: 2 * count], held_ref, up_ref, down_ref, sems)
     inner = dot_nt(low_ref[...], up_ref[...]) + bias_ref[block_ref[step]]
-    bell = jnp.exp(-0.5 * inner * inner)
+    bell = jnp.exp2(inner * inner * (-0.5 * 1.4426950408889634))
     share = normal_share(inner, bell)
     act = (inner * share).astype(BF16)
     act_ref[0] = act

time: 809 us -> 808 us (level)
  transfers between devices with their start and end apart: 126 -> 126, of which waited for: 50 -> 48; matrix products, arithmetic and copies ran while one was open for 16% -> 16% of each run, Pallas kernels for 25% -> 24%
where the time goes in v1:
time: 808 us; the launch traced here: 796 us
  Pallas kernels  261 us (32%)
  waiting for transfers between devices  217 us (27%)
  other arithmetic  105 us (13%)
  starting transfers between devices  99 us (12%)
  local copies, waits for them, and re-layouts  80.9 us (10%)
  matrix products  28.2 us (3%)
    ppermute x89, waiting for transfers between devices, send(): return lax.ppermute(value, 'wide', LINKS[link])  203 us
    ppermute x89, starting transfers between devices, send(): return lax.ppermute(value, 'wide', LINKS[link])  92.1 us
    pallas_call x2, Pallas kernels, highway_backward(): pl.pallas_call(partial(highway_backward_kernel, layout), grid_spec=pltpu....  42.7 us
    pallas_call x12, Pallas kernels, highway_weight_gradient(): pl.pallas_call(weight_kernel, grid_spec=pltpu.PrefetchScalarGridSpec(num_...  40.9 us
    pallas_call x2, Pallas kernels, highway_forward(): pl.pallas_call(partial(highway_forward_kernel, layout), grid_spec=pltpu.P...  38.9 us
    unnamed x400, local copies, waits for them, and re-layouts  37.8 us
    pallas_call x1, Pallas kernels, conv_backward(): pl.pallas_call(conv_backward_kernel, out_shape=(jax.ShapeDtypeStruct((fil...  31.6 us
    pallas_call x1, Pallas kernels, feed_forward_back(): pl.pallas_call(partial(feed_forward_back_kernel, len(up)), grid_spec=pltp...  24.3 us
  transfers between devices with their start and end apart: 126, of which 48 were waited for; matrix products, arithmetic and copies ran while one was open for 16% of the time, Pallas kernels for 24%

profile of v1, /device:TPU:0, one launch (start us, length us, event | category | flops | bytes accessed | tf_op | source)
XLA Modules:
  0.0 796.4 jit_solution(17562933542968544333)
XLA Ops:
  37.0 7.2 collective-permute-done.13
  47.0 10.5 %collective-permute-done.10.refs_1_ = bf16[4,352,128]{2,1,0:T(8,128)(2,1)S(1)} collective-permute-done((bf16[4,352,128]{2,1,0:T(8,128)(2,1)S(1)}, bf16[4,352,128]{2,1,0:T(8,128)(2,1)S(1)}, u32[]{:S(2)}, u32[]{:S(2)}) %collective-permute-start.10) | collective-permute-done | bytes 360480 | tf_op jit(solution)/shard_map/ppermute | solution.py:634
  57.5 5.6 collective-permute-done.15
  63.6 5.9 collective-permute-done.12
  74.1 7.8 collective-permute-done.19
  81.9 6.7 collective-permute-done.20
  89.4 8.2 %collective-permute-done.21 = bf16[512,256]{1,0:T(8,128)(2,1)S(1)} collective-permute-done((bf16[512,256]{1,0:T(8,128)(2,1)}, bf16[512,256]{1,0:T(8,128)(2,1)S(1)}, u32[]{:S(2)}, u32[]{:S(2)}) %collective-permute-start.21) | collective-permute-done | bytes 262176 | tf_op jit(solution)/shard_map/ppermute | solution.py:634
  97.7 4.9 embed.1.g_ref
  115.5 11.2 %conv_forward.1.h_ref = f32[512,2048]{1,0:T(8,128)S(1)} custom-call(s32[8]{0:T(128)S(1)} %pad_add_fusion.scalar_ref, s32[816]{0:T(1024)S(1)} %fusion.76.tile_ref, s32[816]{0:T(1024)S(1)} %subtract_select_fusion.pos_ref, bf16[8,512,128]{2,1,0:T(8,128)(2,1)S(1)} %copy-done.57, bf16[128,2048]{1,0:T(8,128)(2,1)S(1)} %or_select_fusion.w_ref, ...), custom_call_target="tpu_custom_call" | custom-call | flops 17600000000 | bytes 48000000 | tf_op jit(solution)/shard_map/conv_forward/pallas_call | solution.py:175
  128.7 12.1 %collective-permute-done.32.refs_1_ = bf16[4,160,768]{2,1,0:T(8,128)(2,1)S(1)} collective-permute-done((bf16[4,160,768]{2,1,0:T(8,128)(2,1)S(1)}, bf16[4,160,768]{2,1,0:T(8,128)(2,1)S(1)}, u32[]{:S(2)}, u32[]{:S(2)}) %collective-permute-start.32) | collective-permute-done | bytes 983072 | tf_op jit(solution)/shard_map/ppermute | solution.py:634
  153.3 7.4 collective-permute-done.27
  181.1 19.5 %highway_forward.2 = (f32[512,2048]{1,0:T(8,128)}, f32[512,2048]{1,0:T(8,128)}, f32[512,2048]{1,0:T(8,128)}, bf16[512,2048]{1,0:T(8,128)(2,1)}) custom-call(s32[8]{0:T(128)} %get-tuple-element.1014.place_ref, s32[8]{0:T(128)} %get-tuple-element.1013.select_ref, s32[1]{0:T(128)} %bitcast.core_ref.which_ref, f32[512,2048]{1,0:T(8,128)} %copy-done.59, ...), custom_call_target="tpu_custom_call" | custom-call | flops 20899999744 | bytes 57000000 | tf_op jit(solution)/shard_map/highway_forward/pallas_call | solution.py:385
  200.6 4.7 collective-permute-done.41.refs_2_
  223.6 15.1 %collective-permute-done.45.refs_3_ = bf16[4,160,768]{2,1,0:T(8,128)(2,1)} collective-permute-done((bf16[4,160,768]{2,1,0:T(8,128)(2,1)}, bf16[4,160,768]{2,1,0:T(8,128)(2,1)}, u32[]{:S(2)}, u32[]{:S(2)}) %collective-permute-start.45) | collective-permute-done | bytes 983072 | tf_op jit(solution)/shard_map/ppermute | solution.py:634
  257.8 19.4 %highway_forward.3 = (f32[512,2048]{1,0:T(8,128)}, f32[512,2048]{1,0:T(8,128)}, f32[512,2048]{1,0:T(8,128)}, bf16[512,2048]{1,0:T(8,128)(2,1)}) custom-call(s32[8]{0:T(128)} %get-tuple-element.1014.place_ref, s32[8]{0:T(128)} %get-tuple-element.1013.select_ref, s32[1]{0:T(128)} %bitcast.core_ref.which_ref, f32[512,2048]{1,0:T(8,128)} %get-tuple-element.590.h_ref, ...), custom_call_target="tpu_custom_call" | custom-call | flops 20899999744 | bytes 57000000 | tf_op jit(solution)/shard_map/highway_forward/pallas_call | solution.py:385
  286.6 8.4 %place_rows.1 = (bf16[2304,768]{1,0:T(8,128)(2,1)S(1)}, bf16[768,768]{1,0:T(8,128)(2,1)S(1)}, bf16[2048,768]{1,0:T(8,128)(2,1)S(1)}) custom-call(s32[16]{0:T(128)S(1)} %fusion.80.place_ref, s32[1]{0:T(128)} %bitcast.core_ref.which_ref, bf16[4,160,768]{2,1,0:T(8,128)(2,1)S(1)} %pad_maximum_fusion.8.refs_0_, bf16[4,160,768]{2,1,0:T(8,128)(2,1)S(1)} %copy-done.37, ...), custom_call_target="tpu_custom_call" | custom-call | flops 7699999744 | bytes 21000000 | tf_op jit(solution)/shard_map/place_rows/pallas_call | solution.py:560
  314.4 4.6 fusion.query_ref.key_ref.value_ref
  319.2 11.1 %attend.1 = bf16[512,768]{1,0:T(8,128)(2,1)S(1)} custom-call(bf16[512,2304]{1,0:T(8,128)(2,1)S(1)} %fusion.query_ref.key_ref.value_ref, bf16[512,2304]{1,0:T(8,128)(2,1)S(1)} %fusion.query_ref.key_ref.value_ref, bf16[512,2304]{1,0:T(8,128)(2,1)S(1)} %fusion.query_ref.key_ref.value_ref), custom_call_target="tpu_custom_call" | custom-call | flops 13200000000 | bytes 36000000 | tf_op jit(solution)/shard_map/attend/pallas_call | solution.py:1240
  336.1 21.0 %feed_forward.1 = (bf16[8,512,384]{2,1,0:T(8,128)(2,1)}, bf16[8,512,384]{2,1,0:T(8,128)(2,1)}, bf16[512,768]{1,0:T(8,128)(2,1)}, f32[512,768]{1,0:T(8,128)}, f32[8,768]{1,0:T(8,128)}) custom-call(s32[8,2]{1,0:T(8,128)} %add_select_fusion.slot_ref, s32[8]{0:T(128)} %add_add_fusion.2.block_ref, s32[1]{0:T(128)} %bitcast.core_ref.which_ref, ...), custom_call_target="tpu_custom_call" | custom-call | flops 22000001024 | bytes 60000000 | tf_op jit(solution)/shard_map/feed_forward/pallas_call | solution.py:1044
  357.1 24.3 %feed_back.1 = (bf16[2,4,2,96,768]{4,3,2,1,0:T(8,128)(2,1)}, bf16[2,4,2,96,768]{4,3,2,1,0:T(8,128)(2,1)}, bf16[2,4,2,96,768]{4,3,2,1,0:T(8,128)(2,1)}, bf16[2,4,...) custom-call(s32[8,2]{1,0:T(8,128)} %add_select_fusion.slot_ref, ...), custom_call_target="tpu_custom_call" | custom-call | flops 27499999232 | bytes 75000000 | tf_op jit(solution)/shard_map/feed_back/pallas_call | solution.py:1170
  394.4 16.6 %attend_back.1 = (bf16[512,768]{1,0:T(8,128)(2,1)S(1)}, bf16[512,768]{1,0:T(8,128)(2,1)S(1)}, bf16[512,768]{1,0:T(8,128)(2,1)S(1)}) custom-call(bf16[512,2304]{1,0:T(8,128)(2,1)S(1)} %copy-done.55, bf16[512,2304]{1,0:T(8,128)(2,1)S(1)} %copy-done.55, bf16[512,2304]{1,0:T(8,128)(2,1)S(1)} %copy-done.55, bf16[512,768]{1,0:T(8,128)(2,1)S(1)} %convolution_convert_fusion.4.grad_ref), custom_call_target="tpu_custom_call" | custom-call | flops 18699999232 | bytes 51000000 | tf_op jit(solution)/shard_map/attend_back/pallas_call | solution.py:1275
  413.0 8.5 %collective-permute-done.78 = bf16[4,2,96,768]{3,2,1,0:T(8,128)(2,1)S(1)} collective-permute-done((bf16[4,2,96,768]{3,2,1,0:T(8,128)(2,1)S(1)}, bf16[4,2,96,768]{3,2,1,0:T(8,128)(2,1)S(1)}, u32[]{:S(2)}, u32[]{:S(2)}) %collective-permute-start.78) | collective-permute-done | bytes 1179680 | tf_op jit(solution)/shard_map/ppermute | solution.py:634
  432.6 6.6 fusion.26.grad_ref
  448.1 21.2 %highway_backward.2 = (bf16[2,512,2048]{2,1,0:T(8,128)(2,1)}, f32[2,1,2048]{2,1,0:T(1,128)}, f32[512,2048]{1,0:T(8,128)}) custom-call(s32[8]{0:T(128)} %get-tuple-element.1014.place_ref, s32[8]{0:T(128)} %get-tuple-element.1013.select_ref, s32[1]{0:T(128)} %bitcast.core_ref.which_ref, f32[512,2048]{1,0:T(8,128)} %fusion.26.grad_ref, ...), custom_call_target="tpu_custom_call" | custom-call | flops 23100000256 | bytes 63000000 | tf_op jit(solution)/shard_map/highway_backward/pallas_call | solution.py:449
  521.1 21.5 %highway_backward.3 = (bf16[2,512,2048]{2,1,0:T(8,128)(2,1)}, f32[2,1,2048]{2,1,0:T(1,128)}, f32[512,2048]{1,0:T(8,128)}) custom-call(s32[8]{0:T(128)} %get-tuple-element.1014.place_ref, s32[8]{0:T(128)} %get-tuple-element.1013.select_ref, s32[1]{0:T(128)} %bitcast.core_ref.which_ref, f32[512,2048]{1,0:T(8,128)} %get-tuple-element.745.grad_ref, ...), custom_call_target="tpu_custom_call" | custom-call | flops 23100000256 | bytes 63000000 | tf_op jit(solution)/shard_map/highway_backward/pallas_call | solution.py:449
  573.5 31.6 %conv_backward.1 = (bf16[2048,128]{1,0:T(8,128)(2,1)S(1)}, f32[8,512,128]{2,1,0:T(8,128)S(1)}) custom-call(s32[8]{0:T(128)S(1)} %copy-done.47, s32[816]{0:T(1024)S(1)} %copy-done.32, s32[816]{0:T(1024)S(1)} %copy-done.34, bf16[8,512,128]{2,1,0:T(8,128)(2,1)S(1)} %copy-done.58, bf16[128,2048]{1,0:T(8,128)(2,1)S(1)} %copy-done.26, s32[512,1]{1,0:T(8,128)S(1)} %copy-done.30, ...), custom_call_target="tpu_custom_call" | custom-call | flops 38499999744 | bytes 105000000 | tf_op jit(solution)/shard_map/conv_backward/pallas_call | solution.py:232
  624.2 4.4 table.1
  665.5 8.8 %collective-permute-done.101 = bf16[4,2,512,128]{3,2,1,0:T(8,128)(2,1)S(1)} collective-permute-done((bf16[4,2,512,128]{3,2,1,0:T(8,128)(2,1)S(1)}, bf16[4,2,512,128]{3,2,1,0:T(8,128)(2,1)S(1)}, u32[]{:S(2)}, u32[]{:S(2)}) %collective-permute-start.101) | collective-permute-done | bytes 1048608 | tf_op jit(solution)/shard_map/ppermute | solution.py:634
  691.2 24.9 %collective-permute-done.107 = bf16[4,512,128]{2,1,0:T(8,128)(2,1)} collective-permute-done((bf16[4,512,128]{2,1,0:T(8,128)(2,1)}, bf16[4,512,128]{2,1,0:T(8,128)(2,1)}, u32[]{:S(2)}, u32[]{:S(2)}) %collective-permute-start.107) | collective-permute-done | bytes 524320 | tf_op jit(solution)/shard_map/ppermute | solution.py:634
  727.3 5.6 collective-permute-done.114
  745.8 12.3 %collective-permute-done.115 = bf16[1024,128]{1,0:T(8,128)(2,1)S(1)} collective-permute-done((bf16[1024,128]{1,0:T(8,128)(2,1)S(1)}, bf16[1024,128]{1,0:T(8,128)(2,1)S(1)}, u32[]{:S(2)}, u32[]{:S(2)}) %collective-permute-start.115) | collective-permute-done | bytes 262176 | tf_op jit(solution)/shard_map/ppermute | solution.py:634
  767.3 12.5 %collective-permute-done.124 = f32[224,128]{1,0:T(8,128)S(1)} collective-permute-done((f32[224,128]{1,0:T(8,128)S(1)}, f32[224,128]{1,0:T(8,128)S(1)}, u32[]{:S(2)}, u32[]{:S(2)}) %collective-permute-start.124) | collective-permute-done | bytes 114720 | tf_op jit(solution)/shard_map/ppermute | solution.py:634
  (908 shorter events, 401.2 us)
Async XLA Ops:
  29.9 40.0 %collective-permute-start.22 = (bf16[4,512,256]{2,1,0:T(8,128)(2,1)S(1)}, bf16[4,512,256]{2,1,0:T(8,128)(2,1)S(1)}, u32[]{:S(2)}, u32[]{:S(2)}) collective-permute-start(bf16[4,512,256]{2,1,0:T(8,128)(2,1)S(1)} %pad_maximum_fusion.4), channel_id=1, source_target_pairs={{0,16},{16,0},{1,17},{17,1},{2,18},{18,2},{3,19},{19,3},{4,20},{20... | collective-permute-start | bytes 3145736 | tf_op jit(solution)/shard_map/ppermute | solution.py:633
  30.0 39.8 %collective-permute-start.8 = (bf16[4,512,256]{2,1,0:T(8,128)(2,1)S(1)}, bf16[4,512,256]{2,1,0:T(8,128)(2,1)S(1)}, u32[]{:S(2)}, u32[]{:S(2)}) collective-permute-start(bf16[4,512,256]{2,1,0:T(8,128)(2,1)S(1)} %pad_maximum_fusion.4), channel_id=1, source_target_pairs={{0,1},{1,0},{2,3},{3,2},{4,5},{5,4},{6,7},{7,6},{8,9},{9,8},{10,11... | collective-permute-start | bytes 3145736 | tf_op jit(solution)/shard_map/ppermute | solution.py:634
  31.6 38.3 %collective-permute-start.9 = (bf16[4,512,256]{2,1,0:T(8,128)(2,1)S(1)}, bf16[4,512,256]{2,1,0:T(8,128)(2,1)}, u32[]{:S(2)}, u32[]{:S(2)}) collective-permute-start(bf16[4,512,256]{2,1,0:T(8,128)(2,1)S(1)} %pad_maximum_fusion.4), channel_id=1, source_target_pairs={{0,2},{1,3},{2,0},{3,1},{4,6},{5,7},{6,4},{7,5},{8,10},{9,11},{10,... | collective-permute-start | bytes 3145736 | tf_op jit(solution)/shard_map/ppermute | solution.py:634
  72.5 35.1 %collective-permute-start.16 = (bf16[4,512,256]{2,1,0:T(8,128)(2,1)}, bf16[4,512,256]{2,1,0:T(8,128)(2,1)}, u32[]{:S(2)}, u32[]{:S(2)}) collective-permute-start(bf16[4,512,256]{2,1,0:T(8,128)(2,1)} %pad_maximum_fusion.5), channel_id=1, source_target_pairs={{0,1},{1,0},{2,3},{3,2},{4,5},{5,4},{6,7},{7,6},{8,9},{9,8},{10,11... | collective-permute-start | bytes 3145736 | tf_op jit(solution)/shard_map/ppermute | solution.py:634
  73.0 34.6 %collective-permute-start.17 = (bf16[4,512,256]{2,1,0:T(8,128)(2,1)}, bf16[4,512,256]{2,1,0:T(8,128)(2,1)}, u32[]{:S(2)}, u32[]{:S(2)}) collective-permute-start(bf16[4,512,256]{2,1,0:T(8,128)(2,1)} %pad_maximum_fusion.5), channel_id=1, source_target_pairs={{0,2},{1,3},{2,0},{3,1},{4,6},{5,7},{6,4},{7,5},{8,10},{9,11},{10,... | collective-permute-start | bytes 3145736 | tf_op jit(solution)/shard_map/ppermute | solution.py:634
  73.5 34.1 %collective-permute-start.24 = (bf16[4,512,256]{2,1,0:T(8,128)(2,1)}, bf16[4,512,256]{2,1,0:T(8,128)(2,1)}, u32[]{:S(2)}, u32[]{:S(2)}) collective-permute-start(bf16[4,512,256]{2,1,0:T(8,128)(2,1)} %collective-permute-done.9), channel_id=1, source_target_pairs={{0,16},{16,0},{1,17},{17,1},{2,18},{18,2},{3,19},{19,3},{4,20},{20... | collective-permute-start | bytes 3145736 | tf_op jit(solution)/shard_map/ppermute | solution.py:633
  73.6 34.1 %collective-permute-start.33 = (bf16[4,512,256]{2,1,0:T(8,128)(2,1)}, bf16[4,512,256]{2,1,0:T(8,128)(2,1)}, u32[]{:S(2)}, u32[]{:S(2)}) collective-permute-start(bf16[4,512,256]{2,1,0:T(8,128)(2,1)} %pad_maximum_fusion.5), channel_id=1, source_target_pairs={{0,16},{16,0},{1,17},{17,1},{2,18},{18,2},{3,19},{19,3},{4,20},{20... | collective-permute-start | bytes 3145736 | tf_op jit(solution)/shard_map/ppermute | solution.py:633
  114.4 26.5 %collective-permute-start.30 = (bf16[4,512,256]{2,1,0:T(8,128)(2,1)S(1)}, bf16[4,512,256]{2,1,0:T(8,128)(2,1)S(1)}, u32[]{:S(2)}, u32[]{:S(2)}) collective-permute-start(bf16[4,512,256]{2,1,0:T(8,128)(2,1)S(1)} %copy-done.161), channel_id=1, source_target_pairs={{0,2},{1,3},{2,0},{3,1},{4,6},{5,7},{6,4},{7,5},{8,10},{9,11},{10,... | collective-permute-start | bytes 3145736 | tf_op jit(solution)/shard_map/ppermute | solution.py:634
  177.8 27.5 %collective-permute-start.39 = (bf16[4,512,256]{2,1,0:T(8,128)(2,1)S(1)}, bf16[4,512,256]{2,1,0:T(8,128)(2,1)S(1)}, u32[]{:S(2)}, u32[]{:S(2)}) collective-permute-start(bf16[4,512,256]{2,1,0:T(8,128)(2,1)S(1)} %pad_maximum_fusion.7), channel_id=1, source_target_pairs={{0,1},{1,0},{2,3},{3,2},{4,5},{5,4},{6,7},{7,6},{8,9},{9,8},{10,11... | collective-permute-start | bytes 3145736 | tf_op jit(solution)/shard_map/ppermute | solution.py:634
  178.4 26.9 %collective-permute-start.40 = (bf16[4,512,256]{2,1,0:T(8,128)(2,1)S(1)}, bf16[4,512,256]{2,1,0:T(8,128)(2,1)}, u32[]{:S(2)}, u32[]{:S(2)}) collective-permute-start(bf16[4,512,256]{2,1,0:T(8,128)(2,1)S(1)} %pad_maximum_fusion.7), channel_id=1, source_target_pairs={{0,2},{1,3},{2,0},{3,1},{4,6},{5,7},{6,4},{7,5},{8,10},{9,11},{10,... | collective-permute-start | bytes 3145736 | tf_op jit(solution)/shard_map/ppermute | solution.py:634
  211.1 27.6 %collective-permute-start.43 = (bf16[4,512,256]{2,1,0:T(8,128)(2,1)}, bf16[4,512,256]{2,1,0:T(8,128)(2,1)}, u32[]{:S(2)}, u32[]{:S(2)}) collective-permute-start(bf16[4,512,256]{2,1,0:T(8,128)(2,1)} %collective-permute-done.25), channel_id=1, source_target_pairs={{0,2},{1,3},{2,0},{3,1},{4,6},{5,7},{6,4},{7,5},{8,10},{9,11},{10,... | collective-permute-start | bytes 3145736 | tf_op jit(solution)/shard_map/ppermute | solution.py:634
  211.6 27.1 %collective-permute-start.44 = (bf16[4,512,256]{2,1,0:T(8,128)(2,1)}, bf16[4,512,256]{2,1,0:T(8,128)(2,1)}, u32[]{:S(2)}, u32[]{:S(2)}) collective-permute-start(bf16[4,512,256]{2,1,0:T(8,128)(2,1)} %collective-permute-done.40), channel_id=1, source_target_pairs={{0,1},{1,0},{2,3},{3,2},{4,5},{5,4},{6,7},{7,6},{8,9},{9,8},{10,11... | collective-permute-start | bytes 3145736 | tf_op jit(solution)/shard_map/ppermute | solution.py:634
  278.3 28.9 %collective-permute-start.68 = (bf16[4,96,768]{2,1,0:T(8,128)(2,1)S(1)}, bf16[4,96,768]{2,1,0:T(8,128)(2,1)S(1)}, u32[]{:S(2)}, u32[]{:S(2)}) collective-permute-start(bf16[4,96,768]{2,1,0:T(8,128)(2,1)S(1)} %pad_maximum_fusion.9.refs_0_), channel_id=1, source_target_pairs={{0,16},{16,0},{1,17},{17,1},{2,18},{18,2},{3,19},{19,3},{4,20},{20... | collective-permute-start | bytes 1769480 | tf_op jit(solution)/shard_map/ppermute | solution.py:633
  279.0 26.7 %collective-permute-start.62 = (bf16[4,96,768]{2,1,0:T(8,128)(2,1)S(1)}, bf16[4,96,768]{2,1,0:T(8,128)(2,1)S(1)}, u32[]{:S(2)}, u32[]{:S(2)}) collective-permute-start(bf16[4,96,768]{2,1,0:T(8,128)(2,1)S(1)} %pad_maximum_fusion.9.refs_0_), channel_id=1, source_target_pairs={{0,1},{1,0},{2,3},{3,2},{4,5},{5,4},{6,7},{7,6},{8,9},{9,8},{10,11... | collective-permute-start | bytes 1769480 | tf_op jit(solution)/shard_map/ppermute | solution.py:634
  393.2 28.3 %collective-permute-start.78 = (bf16[4,2,96,768]{3,2,1,0:T(8,128)(2,1)S(1)}, bf16[4,2,96,768]{3,2,1,0:T(8,128)(2,1)S(1)}, u32[]{:S(2)}, u32[]{:S(2)}) collective-permute-start(bf16[4,2,96,768]{3,2,1,0:T(8,128)(2,1)S(1)} %fusion.6), channel_id=1, source_target_pairs={{0,2},{1,3},{2,0},{3,1},{4,6},{5,7},{6,4},{7,5},{8,10},{9,11},{10,... | collective-permute-start | bytes 3538952 | tf_op jit(solution)/shard_map/ppermute | solution.py:634
  393.8 28.0 %collective-permute-start.79 = (bf16[4,2,96,768]{3,2,1,0:T(8,128)(2,1)S(1)}, bf16[4,2,96,768]{3,2,1,0:T(8,128)(2,1)S(1)}, u32[]{:S(2)}, u32[]{:S(2)}) collective-permute-start(bf16[4,2,96,768]{3,2,1,0:T(8,128)(2,1)S(1)} %fusion.7), channel_id=1, source_target_pairs={{0,1},{1,0},{2,3},{3,2},{4,5},{5,4},{6,7},{7,6},{8,9},{9,8},{10,11... | collective-permute-start | bytes 3538952 | tf_op jit(solution)/shard_map/ppermute | solution.py:634
  513.8 38.9 %collective-permute-start.88 = (bf16[16,176,768]{2,1,0:T(8,128)(2,1)}, bf16[16,176,768]{2,1,0:T(8,128)(2,1)}, u32[]{:S(2)}, u32[]{:S(2)}) collective-permute-start(bf16[16,176,768]{2,1,0:T(8,128)(2,1)} %pad_maximum_fusion.1), channel_id=1, source_target_pairs={{0,16},{16,0},{1,17},{17,1},{2,18},{18,2},{3,19},{19,3},{4,20},{20... | collective-permute-start | bytes 12976136 | tf_op jit(solution)/shard_map/ppermute | solution.py:633
  518.0 34.7 %collective-permute-start.86 = (bf16[4,2,512,128]{3,2,1,0:T(8,128)(2,1)}, bf16[4,2,512,128]{3,2,1,0:T(8,128)(2,1)}, u32[]{:S(2)}, u32[]{:S(2)}) collective-permute-start(bf16[4,2,512,128]{3,2,1,0:T(8,128)(2,1)} %dynamic-slice_bitcast_fusion.8), channel_id=1, source_target_pairs={{0,2},{1,3},{2,0},{3,1},{4,6},{5,7},{6,4},{7,5},{8,10},{9,11},{10,... | collective-permute-start | bytes 3145736 | tf_op jit(solution)/shard_map/ppermute | solution.py:634
  519.4 33.3 %collective-permute-start.87 = (bf16[4,2,512,128]{3,2,1,0:T(8,128)(2,1)S(1)}, bf16[4,2,512,128]{3,2,1,0:T(8,128)(2,1)}, u32[]{:S(2)}, u32[]{:S(2)}) collective-permute-start(bf16[4,2,512,128]{3,2,1,0:T(8,128)(2,1)S(1)} %copy-done.84), channel_id=1, source_target_pairs={{0,1},{1,0},{2,3},{3,2},{4,5},{5,4},{6,7},{7,6},{8,9},{9,8},{10,11... | collective-permute-start | bytes 3145736 | tf_op jit(solution)/shard_map/ppermute | solution.py:634
  520.9 31.8 %collective-permute-start.89 = (bf16[192,768]{1,0:T(8,128)(2,1)}, bf16[192,768]{1,0:T(8,128)(2,1)S(1)}, u32[]{:S(2)}, u32[]{:S(2)}) collective-permute-start(bf16[192,768]{1,0:T(8,128)(2,1)} %fusion.30), channel_id=1, source_target_pairs={{0,4},{1,5},{2,6},{3,7},{4,8},{5,9},{6,10},{7,11},{8,12},{9,13},{1... | collective-permute-start | bytes 884744 | tf_op jit(solution)/shard_map/ppermute | solution.py:634
  567.5 41.1 %collective-permute-start.90 = (bf16[16,1024,128]{2,1,0:T(8,128)(2,1)}, bf16[16,1024,128]{2,1,0:T(8,128)(2,1)}, u32[]{:S(2)}, u32[]{:S(2)}) collective-permute-start(bf16[16,1024,128]{2,1,0:T(8,128)(2,1)} %highway_weight.17), channel_id=1, source_target_pairs={{0,16},{16,0},{1,17},{17,1},{2,18},{18,2},{3,19},{19,3},{4,20},{20... | collective-permute-start | bytes 12582920 | tf_op jit(solution)/shard_map/ppermute | solution.py:633
  567.6 41.1 %collective-permute-start.91 = (bf16[16,1024,128]{2,1,0:T(8,128)(2,1)}, bf16[16,1024,128]{2,1,0:T(8,128)(2,1)}, u32[]{:S(2)}, u32[]{:S(2)}) collective-permute-start(bf16[16,1024,128]{2,1,0:T(8,128)(2,1)} %highway_weight.18), channel_id=1, source_target_pairs={{0,16},{16,0},{1,17},{17,1},{2,18},{18,2},{3,19},{19,3},{4,20},{20... | collective-permute-start | bytes 12582920 | tf_op jit(solution)/shard_map/ppermute | solution.py:633
  569.1 39.6 %collective-permute-start.92 = (bf16[4,2,512,128]{3,2,1,0:T(8,128)(2,1)}, bf16[4,2,512,128]{3,2,1,0:T(8,128)(2,1)S(1)}, u32[]{:S(2)}, u32[]{:S(2)}) collective-permute-start(bf16[4,2,512,128]{3,2,1,0:T(8,128)(2,1)} %dynamic-slice_bitcast_fusion.6), channel_id=1, source_target_pairs={{0,2},{1,3},{2,0},{3,1},{4,6},{5,7},{6,4},{7,5},{8,10},{9,11},{10,... | collective-permute-start | bytes 3145736 | tf_op jit(solution)/shard_map/ppermute | solution.py:634
  569.8 38.9 %collective-permute-start.93 = (bf16[4,2,512,128]{3,2,1,0:T(8,128)(2,1)}, bf16[4,2,512,128]{3,2,1,0:T(8,128)(2,1)S(1)}, u32[]{:S(2)}, u32[]{:S(2)}) collective-permute-start(bf16[4,2,512,128]{3,2,1,0:T(8,128)(2,1)} %dynamic-slice_bitcast_fusion.5), channel_id=1, source_target_pairs={{0,1},{1,0},{2,3},{3,2},{4,5},{5,4},{6,7},{7,6},{8,9},{9,8},{10,11... | collective-permute-start | bytes 3145736 | tf_op jit(solution)/shard_map/ppermute | solution.py:634
  570.3 38.3 %collective-permute-start.94 = (bf16[2,2,176,768]{3,2,1,0:T(8,128)(2,1)}, bf16[2,2,176,768]{3,2,1,0:T(8,128)(2,1)S(1)}, u32[]{:S(2)}, u32[]{:S(2)}) collective-permute-start(bf16[2,2,176,768]{3,2,1,0:T(8,128)(2,1)} %fusion.11), channel_id=1, source_target_pairs={{0,4},{1,5},{2,6},{3,7},{4,8},{5,9},{6,10},{7,11},{8,12},{9,13},{1... | collective-permute-start | bytes 3244040 | tf_op jit(solution)/shard_map/ppermute | solution.py:634
  616.1 28.4 %collective-permute-start.95 = (bf16[4,512,128]{2,1,0:T(8,128)(2,1)}, bf16[4,512,128]{2,1,0:T(8,128)(2,1)}, u32[]{:S(2)}, u32[]{:S(2)}) collective-permute-start(bf16[4,512,128]{2,1,0:T(8,128)(2,1)} %fusion.22), channel_id=1, source_target_pairs={{0,1},{1,0},{2,3},{3,2},{4,5},{5,4},{6,7},{7,6},{8,9},{9,8},{10,11... | collective-permute-start | bytes 1572872 | tf_op jit(solution)/shard_map/ppermute | solution.py:634
  622.6 26.4 %collective-permute-start.99 = (bf16[2,2,176,768]{3,2,1,0:T(8,128)(2,1)}, bf16[2,2,176,768]{3,2,1,0:T(8,128)(2,1)}, u32[]{:S(2)}, u32[]{:S(2)}) collective-permute-start(bf16[2,2,176,768]{3,2,1,0:T(8,128)(2,1)} %fusion.2), channel_id=1, source_target_pairs={{0,4},{1,5},{2,6},{3,7},{4,8},{5,9},{6,10},{7,11},{8,12},{9,13},{1... | collective-permute-start | bytes 3244040 | tf_op jit(solution)/shard_map/ppermute | solution.py:634
  680.0 36.1 %collective-permute-start.106 = (bf16[4,2,576,128]{3,2,1,0:T(8,128)(2,1)}, bf16[4,2,576,128]{3,2,1,0:T(8,128)(2,1)}, u32[]{:S(2)}, u32[]{:S(2)}) collective-permute-start(bf16[4,2,576,128]{3,2,1,0:T(8,128)(2,1)} %fusion.5), channel_id=1, source_target_pairs={{0,1},{1,0},{2,3},{3,2},{4,5},{5,4},{6,7},{7,6},{8,9},{9,8},{10,11... | collective-permute-start | bytes 3538952 | tf_op jit(solution)/shard_map/ppermute | solution.py:634
  681.0 35.0 %collective-permute-start.105 = (bf16[4,2,512,128]{3,2,1,0:T(8,128)(2,1)}, bf16[4,2,512,128]{3,2,1,0:T(8,128)(2,1)}, u32[]{:S(2)}, u32[]{:S(2)}) collective-permute-start(bf16[4,2,512,128]{3,2,1,0:T(8,128)(2,1)} %dynamic-slice_bitcast_fusion.2), channel_id=1, source_target_pairs={{0,2},{1,3},{2,0},{3,1},{4,6},{5,7},{6,4},{7,5},{8,10},{9,11},{10,... | collective-permute-start | bytes 3145736 | tf_op jit(solution)/shard_map/ppermute | solution.py:634
  681.7 34.4 %collective-permute-start.107 = (bf16[4,512,128]{2,1,0:T(8,128)(2,1)}, bf16[4,512,128]{2,1,0:T(8,128)(2,1)}, u32[]{:S(2)}, u32[]{:S(2)}) collective-permute-start(bf16[4,512,128]{2,1,0:T(8,128)(2,1)} %fusion.18), channel_id=1, source_target_pairs={{0,1},{1,0},{2,3},{3,2},{4,5},{5,4},{6,7},{7,6},{8,9},{9,8},{10,11... | collective-permute-start | bytes 1572872 | tf_op jit(solution)/shard_map/ppermute | solution.py:634
  682.9 33.1 %collective-permute-start.108 = (bf16[4,512,128]{2,1,0:T(8,128)(2,1)}, bf16[4,512,128]{2,1,0:T(8,128)(2,1)}, u32[]{:S(2)}, u32[]{:S(2)}) collective-permute-start(bf16[4,512,128]{2,1,0:T(8,128)(2,1)} %fusion.17), channel_id=1, source_target_pairs={{0,2},{1,3},{2,0},{3,1},{4,6},{5,7},{6,4},{7,5},{8,10},{9,11},{10,... | collective-permute-start | bytes 1572872 | tf_op jit(solution)/shard_map/ppermute | solution.py:634
  686.5 29.6 %collective-permute-start.109 = (bf16[2048,128]{1,0:T(8,128)(2,1)}, bf16[2048,128]{1,0:T(8,128)(2,1)}, u32[]{:S(2)}, u32[]{:S(2)}) collective-permute-start(bf16[2048,128]{1,0:T(8,128)(2,1)} %pad_maximum_fusion.11), channel_id=1, source_target_pairs={{0,4},{1,5},{2,6},{3,7},{4,8},{5,9},{6,10},{7,11},{8,12},{9,13},{1... | collective-permute-start | bytes 1572872 | tf_op jit(solution)/shard_map/ppermute | solution.py:634
  (284 other events, 3684.2 us)
